TPU v7x, 32 devices: a whole 2x2x4 slice. The times are simulated.
32 devices in a mesh: section: 2 (over z_hi), tensor: 2 (over z_lo), ctx: 8 (over y, x, core).
Axes of the slice: x: 2, y: 2, z: 4 (z_hi: 2, z_lo: 2; z = z_hi * 2 + z_lo), core: 2. Of those that a mesh axis runs over, the one named last changes fastest.
Arguments:
- inputs: bfloat16 [2, 1024, 2048], P(None, ('tensor', 'ctx')), may hold values from -6 to 6
- cotangent: bfloat16 [2, 1024, 2048], P(None, ('tensor', 'ctx')), may hold values from -6 to 6
- slot_order: int32 [2, 8], replicated, may hold values from 0 to 7, each once within a row
- query_weight: bfloat16 [2, 2048, 1280], P('section', 'ctx', 'tensor'), may hold values from -0.125 to 0.125
- key_value_matrix: bfloat16 [2, 2048, 640], P('section', ('tensor', 'ctx')), may hold values from -0.125 to 0.125
- out_weight: bfloat16 [2, 1280, 2048], P('section', 'tensor', 'ctx'), may hold values from -0.625 to 0.625
- gateup_weight: bfloat16 [2, 2048, 2, 5120], P('section', 'ctx', None, 'tensor'), may hold values from -0.125 to 0.125
- down_weight: bfloat16 [2, 5120, 2048], P('section', 'tensor', 'ctx'), may hold values from -0.078125 to 0.078125
- norm_gains: bfloat16 [2, 4224], P('section', ('tensor', 'ctx')), may hold values from 0.5 to 1.5
Outputs:
- section_out: bfloat16 [2, 2, 1024, 2048], P('section', None, ('tensor', 'ctx'))
- input_grads: bfloat16 [2, 2, 1024, 2048], P('section', None, ('tensor', 'ctx'))
- grad_query: float32 [2, 2048, 1280], P('section', 'ctx', 'tensor')
- grad_keyval: float32 [2, 2048, 640], P('section', ('tensor', 'ctx'))
- grad_out: float32 [2, 1280, 2048], P('section', 'tensor', 'ctx')
- grad_gateup: float32 [2, 2048, 2, 5120], P('section', 'ctx', None, 'tensor')
- grad_down: float32 [2, 5120, 2048], P('section', 'tensor', 'ctx')
- grad_gains: float32 [2, 4224], P('section', ('tensor', 'ctx'))
Inputs may be any that keep to these rules, and one draw needn't show every extreme that they name: Each row is a permutation: index c of ctx holds tokens slot_order[b, c] * 128 to slot_order[b, c] * 128 + 127 of sequence b.
All inputs are finite; a program needn't handle non-finite values.
Results may differ from a plain program's by a relative error of at most 0.033.
Values may be sent and summed in bfloat16 or wider, within the bound.
A program may use at most 320 MiB of HBM per device.

v0:
```python
import jax
import jax.numpy as jnp
from jax import lax
from jax.sharding import PartitionSpec as P

MODEL_WIDTH = 2048
QUERY_HEADS = 20
KEY_VALUE_HEADS = 5
HEAD_SIZE = 64


EPSILON = 1e-06
ROPE_BASE = 10000.0
START_PEAK = -1e30


def from_behind(x, axis, by):
    devices = lax.axis_size(axis)
    pairs = [(i, i + by) for i in range(devices) if 0 <= i + by < devices]
    return lax.ppermute(x, axis, pairs)


def rope_tables(positions, head_width):
    half_width = head_width // 2
    frequency = ROPE_BASE ** (-(jnp.arange(half_width, dtype=jnp.float32) * 2.0) / head_width)
    angles = positions.astype(jnp.float32)[:, None] * frequency[None, :]
    return (jnp.cos(angles), jnp.sin(angles))


def rope_apply(values, cosine_rows, sine_rows):
    half_width = values.shape[-1] // 2
    first_half = values[..., :half_width]
    second_half = values[..., half_width:]
    cos_part = cosine_rows[:, None, :]
    sin_part = sine_rows[:, None, :]
    return jnp.concatenate(
        [
            first_half * cos_part - second_half * sin_part,
            second_half * cos_part + first_half * sin_part,
        ],
        axis=-1,
    )


def rope_back(incoming, cosine_rows, sine_rows):
    half_width = incoming.shape[-1] // 2
    first_half = incoming[..., :half_width]
    second_half = incoming[..., half_width:]
    cos_part = cosine_rows[:, None, :]
    sin_part = sine_rows[:, None, :]
    return jnp.concatenate(
        [
            first_half * cos_part + second_half * sin_part,
            second_half * cos_part - first_half * sin_part,
        ],
        axis=-1,
    )


def norm_parts(values, scaling):
    inverse = lax.rsqrt(jnp.mean(values * values, axis=-1, keepdims=True) + EPSILON)
    unit_rows = values * inverse
    return (unit_rows * scaling, unit_rows, inverse)


def norm_back(incoming, unit_rows, inverse, scaling):
    scaled = incoming * scaling
    inner = jnp.mean(scaled * unit_rows, axis=-1, keepdims=True)
    gain_grad = jnp.sum((incoming * unit_rows).reshape(-1, unit_rows.shape[-1]), axis=0)
    return (inverse * (scaled - unit_rows * inner), gain_grad)


def row_product(pieces_list, left_index, right_index):
    left_rows = jnp.concatenate([piece[left_index] for piece in pieces_list], axis=0)
    right_rows = jnp.concatenate([piece[right_index] for piece in pieces_list], axis=0)
    return lax.dot_general(
        left_rows, right_rows, (((0,), (0,)), ((), ())), preferred_element_type=jnp.float32
    )


def grads_from(pieces_list):
    grad_down = row_product(pieces_list, 0, 1)
    grad_gateup = row_product(pieces_list, 2, 3)
    grad_outw = row_product(pieces_list, 4, 5)
    grad_query = row_product(pieces_list, 6, 7)
    grad_keyval = row_product(pieces_list, 8, 9)
    grad_gain = pieces_list[0][10]
    for piece in pieces_list[1:]:
        grad_gain = grad_gain + piece[10]
    return (grad_query, grad_outw, grad_gateup, grad_down, grad_keyval, grad_gain)


def per_device(
    inputs,
    cotangent,
    slot_order,
    query_weight,
    key_value_matrix,
    out_weight,
    gateup_weight,
    down_weight,
    norm_gains,
):
    sections = lax.axis_size("section")
    tensors = lax.axis_size("tensor")
    contexts = lax.axis_size("ctx")
    section_id = lax.axis_index("section")
    tensor_id = lax.axis_index("tensor")
    context_id = lax.axis_index("ctx")
    batches = inputs.shape[0]
    rows_halved = inputs.shape[1]
    local_rows = rows_halved * tensors
    seq_rows = local_rows * contexts
    heads_here = query_weight.shape[2] // HEAD_SIZE
    units_here = down_weight.shape[1]
    key_columns = KEY_VALUE_HEADS * HEAD_SIZE
    rows_per_block = min(512, seq_rows)
    number_of_blocks = seq_rows // rows_per_block
    scale_query = HEAD_SIZE ** (-0.5)
    query_group_width = QUERY_HEADS // KEY_VALUE_HEADS
    head_numbers = tensor_id * heads_here + jnp.arange(heads_here)
    head_picker = head_numbers[:, None] // query_group_width == jnp.arange(KEY_VALUE_HEADS)[None, :]
    select_low = head_picker.astype(jnp.bfloat16)
    select_wide = head_picker.astype(jnp.float32)
    row_half = jnp.arange(rows_halved)
    row_local = jnp.arange(local_rows)
    within_seq = jnp.arange(tensors)[:, None, None] * rows_halved + row_half[None, None, :]

    def gather_rows(values):
        return lax.all_gather(values, "tensor", axis=0, tiled=True)

    def scatter_rows(values):
        return lax.psum_scatter(
            values.astype(jnp.bfloat16), "tensor", scatter_dimension=0, tiled=True
        ).astype(jnp.float32)

    def expand(block_part):
        return jnp.einsum(
            "khd,gh->kgd", block_part, select_low, preferred_element_type=jnp.float32
        ).astype(jnp.bfloat16)

    def block_scores(query_low, block_kv, pos_block, query_pos):
        keys_here = expand(block_kv[:, 0])
        scores = jnp.einsum(
            "qgd,kgd->gqk", query_low, keys_here, preferred_element_type=jnp.float32
        )
        allowed = pos_block[None, :] <= query_pos[:, None]
        return (jnp.where(allowed[None], scores, -jnp.inf), keys_here)

    def split_blocks(key_value_gathered, key_pos):
        return (
            key_value_gathered.reshape(
                number_of_blocks, rows_per_block, 2, KEY_VALUE_HEADS, HEAD_SIZE
            ),
            key_pos.reshape(number_of_blocks, rows_per_block),
        )

    def layer_backward(upstream, kept_state, weights):
        (
            attn_unit,
            attn_inv,
            normed_own,
            normed_all,
            query_unit,
            query_inv,
            query_low,
            key_unit,
            key_inv,
            key_value_gathered,
            log_mass,
            mixture,
            mixture_low,
            ffn_unit,
            ffn_inv,
            second_all,
            gateup,
            hidden_low,
            query_cos,
            query_sin,
            own_cos,
            own_sin,
            query_pos,
            key_pos,
        ) = kept_state
        query_full, out_full, gateup_full, down_full, keyval_full, gains_full = weights
        attn_gain = gains_full[:MODEL_WIDTH]
        ffn_gain = gains_full[MODEL_WIDTH : 2 * MODEL_WIDTH]
        query_gain = gains_full[2 * MODEL_WIDTH : 2 * MODEL_WIDTH + HEAD_SIZE]
        key_gain = gains_full[2 * MODEL_WIDTH + HEAD_SIZE :]
        down_all = gather_rows(upstream.astype(jnp.bfloat16))
        hidden_grad = jnp.dot(down_all, down_full.T, preferred_element_type=jnp.float32)
        gate_values = gateup[:, :units_here]
        up_values = gateup[:, units_here:]
        sigmoid_gate = jax.nn.sigmoid(gate_values)
        gate_grad = (
            hidden_grad * up_values * (sigmoid_gate * (1.0 + gate_values * (1.0 - sigmoid_gate)))
        )
        up_grad = hidden_grad * jax.nn.silu(gate_values)
        gateup_low = jnp.concatenate([gate_grad, up_grad], axis=1).astype(jnp.bfloat16)
        normed_grad = scatter_rows(
            jnp.dot(gateup_low, gateup_full.T, preferred_element_type=jnp.float32)
        )
        residual_part, ffn_gain_grad = norm_back(normed_grad, ffn_unit, ffn_inv, ffn_gain)
        middle = upstream + residual_part
        middle_all = gather_rows(middle.astype(jnp.bfloat16))
        mixture_grad = jnp.dot(middle_all, out_full.T, preferred_element_type=jnp.float32)
        mixture_grad_low = mixture_grad.astype(jnp.bfloat16).reshape(
            local_rows, heads_here, HEAD_SIZE
        )
        offsets = jnp.sum(mixture_grad_low.astype(jnp.float32) * mixture, axis=-1).T
        blocks, pos_blocks = split_blocks(key_value_gathered, key_pos)

        def grad_step(query_grad, packed):
            scores, keys_here = block_scores(query_low, packed[0], packed[1], query_pos)
            weights_full = jnp.exp(scores - log_mass[..., None])
            weights_low = weights_full.astype(jnp.bfloat16)
            values_here = expand(packed[0][:, 1])
            weight_grad = jnp.einsum(
                "qgd,kgd->gqk", mixture_grad_low, values_here, preferred_element_type=jnp.float32
            )
            score_low = (weights_full * (weight_grad - offsets[..., None])).astype(jnp.bfloat16)
            query_grad = query_grad + jnp.einsum(
                "gqk,kgd->qgd", score_low, keys_here, preferred_element_type=jnp.float32
            )
            key_grad = jnp.einsum(
                "gqk,qgd->kgd", score_low, query_low, preferred_element_type=jnp.float32
            )
            value_grad = jnp.einsum(
                "gqk,qgd->kgd", weights_low, mixture_grad_low, preferred_element_type=jnp.float32
            )
            pair_rows = jnp.stack(
                [
                    jnp.einsum("kgd,gh->khd", key_grad, select_wide),
                    jnp.einsum("kgd,gh->khd", value_grad, select_wide),
                ],
                axis=1,
            )
            return (query_grad, pair_rows.reshape(rows_per_block, 2 * key_columns))

        query_grad, pair_blocks = lax.scan(
            grad_step,
            jnp.zeros((local_rows, heads_here, HEAD_SIZE), jnp.float32),
            (blocks, pos_blocks),
        )
        key_value_gradient = lax.psum_scatter(
            pair_blocks.reshape(seq_rows, 2 * key_columns),
            ("tensor", "ctx"),
            scatter_dimension=0,
            tiled=True,
        )
        rotated_key_gradient = key_value_gradient[:, :key_columns].reshape(
            rows_halved, KEY_VALUE_HEADS, HEAD_SIZE
        )
        key_raw_grad, key_gain_grad = norm_back(
            rope_back(rotated_key_gradient, own_cos, own_sin), key_unit, key_inv, key_gain
        )
        keyval_low = jnp.concatenate(
            [key_raw_grad.reshape(rows_halved, key_columns), key_value_gradient[:, key_columns:]],
            axis=1,
        ).astype(jnp.bfloat16)
        own_grad = jnp.dot(keyval_low, keyval_full.T, preferred_element_type=jnp.float32)
        query_raw_grad, query_gain_grad = norm_back(
            rope_back(query_grad * scale_query, query_cos, query_sin),
            query_unit,
            query_inv,
            query_gain,
        )
        query_grad_low = query_raw_grad.reshape(local_rows, heads_here * HEAD_SIZE).astype(
            jnp.bfloat16
        )
        normed_grad = (
            scatter_rows(jnp.dot(query_grad_low, query_full.T, preferred_element_type=jnp.float32))
            + own_grad
        )
        residual_part, attn_gain_grad = norm_back(normed_grad, attn_unit, attn_inv, attn_gain)
        gain_grad = jnp.concatenate([attn_gain_grad, ffn_gain_grad, query_gain_grad, key_gain_grad])
        pieces = (
            hidden_low,
            down_all,
            second_all,
            gateup_low,
            mixture_low,
            middle_all,
            normed_all,
            query_grad_low,
            normed_own,
            keyval_low,
            gain_grad,
        )
        return (middle + residual_part, pieces)

    step_count = batches + sections - 1
    query_full = lax.all_gather(query_weight[0], "ctx", axis=0, tiled=True)
    out_full = lax.all_gather(out_weight[0], "ctx", axis=1, tiled=True)
    gateup_full = lax.all_gather(gateup_weight[0], "ctx", axis=0, tiled=True)
    down_full = lax.all_gather(down_weight[0], "ctx", axis=1, tiled=True)
    keyval_full = lax.all_gather(key_value_matrix[0], ("tensor", "ctx"), axis=0, tiled=True)
    gains_full = lax.all_gather(norm_gains[0], ("tensor", "ctx"), axis=0, tiled=True)
    weights_now = (
        query_full,
        out_full,
        gateup_full.reshape(MODEL_WIDTH, 2 * units_here),
        down_full,
        keyval_full,
        gains_full.astype(jnp.float32),
    )
    received = jnp.zeros_like(inputs[0])
    produced = []
    kept_all = []
    for step_index in range(step_count):
        batch_index = jnp.clip(step_index - section_id, 0, batches - 1)
        first_in = inputs[min(step_index, batches - 1)]
        residual = jnp.where(section_id == 0, first_in, received).astype(jnp.float32)
        layer_residual = residual
        (
            layer_query_full,
            layer_out_full,
            layer_gateup_full,
            layer_down_full,
            layer_keyval_full,
            layer_gains_full,
        ) = weights_now
        layer_attn_gain = layer_gains_full[:MODEL_WIDTH]
        layer_ffn_gain = layer_gains_full[MODEL_WIDTH : 2 * MODEL_WIDTH]
        layer_query_gain = layer_gains_full[2 * MODEL_WIDTH : 2 * MODEL_WIDTH + HEAD_SIZE]
        layer_key_gain = layer_gains_full[2 * MODEL_WIDTH + HEAD_SIZE :]
        slot_row = jnp.sum(
            jnp.where(jnp.arange(batches)[:, None] == batch_index, slot_order, 0), axis=0
        )
        own_slot = jnp.sum(jnp.where(jnp.arange(contexts) == context_id, slot_row, 0))
        positions_query_pos = own_slot * local_rows + row_local
        positions_key_pos = (slot_row[None, :, None] * local_rows + within_seq).reshape(seq_rows)
        own_pos = own_slot * local_rows + tensor_id * rows_halved + row_half
        layer_query_cos, layer_query_sin = rope_tables(positions_query_pos, HEAD_SIZE)
        layer_own_cos, layer_own_sin = rope_tables(own_pos, HEAD_SIZE)
        normed, layer_attn_unit, layer_attn_inv = norm_parts(layer_residual, layer_attn_gain)
        layer_normed_own = normed.astype(jnp.bfloat16)
        layer_normed_all = gather_rows(layer_normed_own)
        query_raw = jnp.dot(
            layer_normed_all, layer_query_full, preferred_element_type=jnp.float32
        ).reshape(local_rows, heads_here, HEAD_SIZE)
        query_hat, layer_query_unit, layer_query_inv = norm_parts(query_raw, layer_query_gain)
        layer_query_low = (
            rope_apply(query_hat, layer_query_cos, layer_query_sin) * scale_query
        ).astype(jnp.bfloat16)
        key_value_projected = jnp.dot(
            layer_normed_own, layer_keyval_full, preferred_element_type=jnp.float32
        )
        key_hat, layer_key_unit, layer_key_inv = norm_parts(
            key_value_projected[:, :key_columns].reshape(rows_halved, KEY_VALUE_HEADS, HEAD_SIZE),
            layer_key_gain,
        )
        key_low = (
            rope_apply(key_hat, layer_own_cos, layer_own_sin)
            .astype(jnp.bfloat16)
            .reshape(rows_halved, key_columns)
        )
        keyval_own = jnp.concatenate(
            [key_low, key_value_projected[:, key_columns:].astype(jnp.bfloat16)], axis=1
        )
        layer_key_value_gathered = lax.all_gather(keyval_own, ("tensor", "ctx"), axis=0, tiled=True)
        attend_query_low = layer_query_low
        attend_query_pos = positions_query_pos
        attend_blocks, attend_pos_blocks = split_blocks(layer_key_value_gathered, positions_key_pos)

        def peak_step(carry, packed):
            old_peak, mass_sum = carry
            scores, unused = block_scores(attend_query_low, packed[0], packed[1], attend_query_pos)
            new_peak = jnp.maximum(old_peak, jnp.max(scores, axis=-1))
            mass_sum = mass_sum * jnp.exp(old_peak - new_peak) + jnp.sum(
                jnp.exp(scores - new_peak[..., None]), axis=-1
            )
            return ((new_peak, mass_sum), None)

        initial = (
            jnp.full((heads_here, local_rows), START_PEAK, jnp.float32),
            jnp.zeros((heads_here, local_rows), jnp.float32),
        )
        (peak_value, mass_sum), unused = lax.scan(
            peak_step, initial, (attend_blocks, attend_pos_blocks)
        )
        attend_log_mass = peak_value + jnp.log(mass_sum)

        def value_step(running, packed):
            scores, unused = block_scores(attend_query_low, packed[0], packed[1], attend_query_pos)
            weights_low = jnp.exp(scores - attend_log_mass[..., None]).astype(jnp.bfloat16)
            values_here = expand(packed[0][:, 1])
            return (
                running
                + jnp.einsum(
                    "gqk,kgd->qgd", weights_low, values_here, preferred_element_type=jnp.float32
                ),
                None,
            )

        attend_mixture, unused = lax.scan(
            value_step,
            jnp.zeros((local_rows, heads_here, HEAD_SIZE), jnp.float32),
            (attend_blocks, attend_pos_blocks),
        )
        layer_mixture_low = attend_mixture.reshape(local_rows, heads_here * HEAD_SIZE).astype(
            jnp.bfloat16
        )
        layer_residual = layer_residual + scatter_rows(
            jnp.dot(layer_mixture_low, layer_out_full, preferred_element_type=jnp.float32)
        )
        normed, layer_ffn_unit, layer_ffn_inv = norm_parts(layer_residual, layer_ffn_gain)
        layer_second_all = gather_rows(normed.astype(jnp.bfloat16))
        layer_gateup = jnp.dot(
            layer_second_all, layer_gateup_full, preferred_element_type=jnp.float32
        )
        layer_hidden_low = (
            jax.nn.silu(layer_gateup[:, :units_here]) * layer_gateup[:, units_here:]
        ).astype(jnp.bfloat16)
        result = layer_residual + scatter_rows(
            jnp.dot(layer_hidden_low, layer_down_full, preferred_element_type=jnp.float32)
        )
        layer_kept_state = (
            layer_attn_unit,
            layer_attn_inv,
            layer_normed_own,
            layer_normed_all,
            layer_query_unit,
            layer_query_inv,
            layer_query_low,
            layer_key_unit,
            layer_key_inv,
            layer_key_value_gathered,
            attend_log_mass,
            attend_mixture,
            layer_mixture_low,
            layer_ffn_unit,
            layer_ffn_inv,
            layer_second_all,
            layer_gateup,
            layer_hidden_low,
            layer_query_cos,
            layer_query_sin,
            layer_own_cos,
            layer_own_sin,
            positions_query_pos,
            positions_key_pos,
        )
        result, kept_state = (result, layer_kept_state)
        result_low = result.astype(jnp.bfloat16)
        produced.append(result_low)
        kept_all.append(kept_state)
        if step_index + 1 < step_count:
            received = from_behind(result_low, "section", 1)
    kept_stack = jax.tree.map(lambda *parts: jnp.stack(parts), *kept_all)
    produced_stack = jnp.stack(produced)
    returned = jnp.zeros_like(inputs[0])
    consumed = []
    pieces_all = []
    for step_index in range(step_count):
        source = jnp.clip(step_index - (sections - 1) + 2 * section_id, 0, step_count - 1)
        kept_state = jax.tree.map(
            lambda stacked: lax.dynamic_index_in_dim(stacked, source, 0, keepdims=False), kept_stack
        )
        live_factor = 1.0 if step_index < batches else 0.0
        top_grad = cotangent[min(step_index, batches - 1)].astype(jnp.float32) * live_factor
        upstream = jnp.where(section_id == sections - 1, top_grad, returned.astype(jnp.float32))
        grad_input, pieces = layer_backward(upstream, kept_state, weights_now)
        pieces_all.append(pieces)
        grad_low = grad_input.astype(jnp.bfloat16)
        consumed.append(grad_low)
        if step_index + 1 < step_count:
            returned = from_behind(grad_low, "section", -1)
    full_set = grads_from(pieces_all)
    consumed_stack = jnp.stack(consumed)
    section_result = jnp.stack(
        [
            lax.dynamic_index_in_dim(produced_stack, batch_no + section_id, 0, keepdims=False)
            for batch_no in range(batches)
        ]
    )[None]
    input_result = jnp.stack(
        [
            lax.dynamic_index_in_dim(
                consumed_stack, batch_no + sections - 1 - section_id, 0, keepdims=False
            )
            for batch_no in range(batches)
        ]
    )[None]
    return (
        section_result,
        input_result,
        lax.psum_scatter(
            full_set[0].astype(jnp.bfloat16), "ctx", scatter_dimension=0, tiled=True
        ).astype(jnp.float32)[None],
        lax.psum_scatter(full_set[4], ("tensor", "ctx"), scatter_dimension=0, tiled=True)[None],
        lax.psum_scatter(
            full_set[1].astype(jnp.bfloat16), "ctx", scatter_dimension=1, tiled=True
        ).astype(jnp.float32)[None],
        lax.psum_scatter(
            full_set[2].reshape(MODEL_WIDTH, 2, units_here).astype(jnp.bfloat16),
            "ctx",
            scatter_dimension=0,
            tiled=True,
        ).astype(jnp.float32)[None],
        lax.psum_scatter(
            full_set[3].astype(jnp.bfloat16), "ctx", scatter_dimension=1, tiled=True
        ).astype(jnp.float32)[None],
        lax.psum_scatter(full_set[5], ("tensor", "ctx"), scatter_dimension=0, tiled=True)[None],
    )


def solution(mesh):
    return jax.shard_map(
        per_device,
        mesh=mesh,
        in_specs=(
            P(None, ("tensor", "ctx"), None),
            P(None, ("tensor", "ctx"), None),
            P(),
            P("section", "ctx", "tensor"),
            P("section", ("tensor", "ctx"), None),
            P("section", "tensor", "ctx"),
            P("section", "ctx", None, "tensor"),
            P("section", "tensor", "ctx"),
            P("section", ("tensor", "ctx")),
        ),
        out_specs=(
            P("section", None, ("tensor", "ctx"), None),
            P("section", None, ("tensor", "ctx"), None),
            P("section", "ctx", "tensor"),
            P("section", ("tensor", "ctx"), None),
            P("section", "tensor", "ctx"),
            P("section", "ctx", None, "tensor"),
            P("section", "tensor", "ctx"),
            P("section", ("tensor", "ctx")),
        ),
        check_vma=False,
    )
```

profile of v0, /device:TPU:0, one launch (start us, length us, event | category | flops | bytes accessed | tf_op | source)
XLA Modules:
  0.0 1680.3 jit_solution(17515753112463054378)
XLA Ops:
  15.8 55.2 %all-reduce = bf16[4224]{0:T(1024)(128)(2,1)S(1)} all-reduce(bf16[4224]{0:T(1024)(128)(2,1)S(1)} %dynamic-update-slice), channel_id=2, replica_groups=mesh['section'=2,'tensor'=2,'ctx'=8] {'tensor','ctx'}, use_global_device_ids=true, to_apply=%add | all-reduce | flops 4224 | bytes 16896
  79.8 7.0 all_gather.66
  93.5 15.1 all-gather.15.cloned.1.call-done
  118.7 12.0 while.118
  131.7 8.3 all-gather.25.cloned.1.call-done
  144.6 13.3 reduce-scatter.26.cloned.1.call-done
  161.5 9.0 all_gather.69
  170.5 96.9 %all-gather.27.cloned.1.call-done = bf16[1,2048,2,2560]{3,2,0,1:T(2,128)(2,1)} async-done(((bf16[1,256,2,2560]{3,2,0,1:T(2,128)(2,1)}), bf16[1,2048,2,2560]{3,2,0,1:T(2,128)(2,1)}) %all-gather.27.cloned.1.call-update) | async-done | bytes 20971536 | tf_op jit(solution)/shard_map/all_gather | solution.py:295
  267.4 14.6 copy.243
  282.0 7.0 copy-done
  291.9 42.8 %all-gather.29.cloned.1.call-done = bf16[1,2560,2048]{2,1,0:T(8,128)(2,1)} async-done(((bf16[1,2560,256]{2,1,0:T(8,128)(2,1)}), bf16[1,2560,2048]{2,1,0:T(8,128)(2,1)}) %all-gather.29.cloned.1.call-update) | async-done | bytes 10485776 | tf_op jit(solution)/shard_map/all_gather | solution.py:296
  334.7 6.4 fusion.317
  341.2 14.7 reduce-scatter.28.cloned.1.call-done
  361.3 5.6 collective-permute-done
  376.4 13.0 all_gather.73
  395.4 17.9 %all-gather.17.cloned.1.call-done = bf16[1024,640]{1,0:T(8,128)(2,1)} async-done(((bf16[64,640]{1,0:T(8,128)(2,1)}), bf16[1024,640]{1,0:T(8,128)(2,1)}) %all-gather.17.cloned.1.call-update) | async-done | bytes 1310736 | tf_op jit(solution)/shard_map/all_gather | solution.py:361
  423.5 7.0 while.119
  430.5 17.0 %while.120 = (s32[]{:T(128)}, f32[128,10,64]{0,2,1:T(8,128)}, bf16[2,512,2,5,64]{1,3,4,2,0:T(8,128)(2,1)}, s32[2,512]{1,0:T(2,128)S(1)}, bf16[128,10,64]{0,2,1:T...) while((s32[]{:T(128)}, f32[128,10,64]{0,2,1:T(8,128)}, ...), condition=%wide.region_24.25_spmd.clone, body=%wide.region_23.24_spmd.clone.sunk | while | flops 177176912 | bytes 5944451 | solution.py:396
  452.4 13.7 reduce-scatter.30.cloned.1.call-done
  469.9 8.9 all_gather.74
  478.7 8.8 fusion.580
  491.5 14.7 reduce-scatter.32.cloned.1.call-done
  508.0 5.0 collective-permute-start.1
  529.4 13.3 all_gather.78
  542.7 9.6 all_gather.76
  555.2 7.9 all-gather.19.cloned.1.call-done
  574.6 17.1 %while.122 = (s32[]{:T(128)}, f32[128,10,64]{0,2,1:T(8,128)}, bf16[2,512,2,5,64]{1,3,4,2,0:T(8,128)(2,1)}, s32[2,512]{1,0:T(2,128)S(1)}, bf16[128,10,64]{0,2,1:T...) while((s32[]{:T(128)}, f32[128,10,64]{0,2,1:T(8,128)}, ...), condition=%wide.region_38.39_spmd.clone, body=%wide.region_37.38_spmd.clone.sunk | while | flops 177176912 | bytes 5944451 | solution.py:396
  603.0 5.2 reduce-scatter.34.cloned.1.call-done
  611.2 8.9 all_gather.77
  620.2 8.8 fusion.581
  633.4 7.7 fusion.365
  642.1 11.8 convolution_convert_fusion.21
  676.2 8.3 all_gather.79
  690.7 20.7 %while.123 = (s32[]{:T(128)}, f32[128,10,64]{0,2,1:T(8,128)S(1)}, f32[2,512,640]{2,1,0:T(8,128)}, bf16[2,512,2,5,64]{1,3,4,2,0:T(8,128)(2,1)}, s32[2,512]{1,0:T(...) while((s32[]{:T(128)}, f32[128,10,64]{0,2,1:T(8,128)S(1)}, ...), condition=%wide.region_46.47_spmd.clone.clone.clone, body=%wide.region_45.46_spmd.clone.clone.clone.sunk | while | flops 438993280 | bytes 33381100 | solution.py:240
  728.8 42.8 %reduce-scatter.58.cloned.1.call-done = f32[64,640]{1,0:T(8,128)} async-done(((f32[1024,640]{1,0:T(8,128)}), f32[64,640]{1,0:T(8,128)}) %reduce-scatter.58.cloned.1.call-update) | async-done | bytes 163856
  777.6 9.5 reduce-scatter.40.cloned.1.call-done
  793.0 15.0 collective-permute-done.2
  808.1 8.9 all_gather.80
  817.0 7.9 fusion.363
  826.1 11.9 convolution_convert_fusion.20
  844.3 6.8 reduce-scatter.42.cloned.1.call-done
  854.3 8.9 all_gather.81
  867.8 20.7 %while.124 = (s32[]{:T(128)}, f32[128,10,64]{0,2,1:T(8,128)S(1)}, f32[2,512,640]{2,1,0:T(8,128)}, bf16[2,512,2,5,64]{1,3,4,2,0:T(8,128)(2,1)}, s32[2,512]{1,0:T(...) while((s32[]{:T(128)}, f32[128,10,64]{0,2,1:T(8,128)S(1)}, ...), condition=%wide.region_56.57_spmd.clone.clone.clone, body=%wide.region_55.56_spmd.clone.clone.clone.sunk | while | flops 438993280 | bytes 33381100 | solution.py:240
  893.3 55.0 %reduce-scatter.60.cloned.1.call-done = f32[64,640]{1,0:T(8,128)} async-done(((f32[1024,640]{1,0:T(8,128)}), f32[64,640]{1,0:T(8,128)}) %reduce-scatter.60.cloned.1.call-update) | async-done | bytes 163856
  953.1 11.0 reduce-scatter.44.cloned.1.call-done
  969.5 15.0 collective-permute-done.3
  984.6 9.3 all_gather.82
  994.0 7.9 fusion.361
  1003.0 11.9 convolution_convert_fusion.19
  1018.8 9.1 reduce-scatter.46.cloned.1.call-done
  1031.5 8.9 all_gather.83
  1045.1 20.7 %while.125 = (s32[]{:T(128)}, f32[128,10,64]{0,2,1:T(8,128)S(1)}, f32[2,512,640]{2,1,0:T(8,128)}, bf16[2,512,2,5,64]{1,3,4,2,0:T(8,128)(2,1)}, s32[2,512]{1,0:T(...) while((s32[]{:T(128)}, f32[128,10,64]{0,2,1:T(8,128)S(1)}, ...), condition=%wide.region_66.67_spmd.clone.clone.clone, body=%wide.region_65.66_spmd.clone.clone.clone.sunk | while | flops 438993280 | bytes 33381100 | solution.py:240
  1067.5 6.4 fusion.323
  1090.6 17.0 %convolution_convert_fusion.15 = bf16[2048,5120]{1,0:T(8,128)(2,1)} fusion(bf16[128,2560]{1,0:T(8,128)(2,1)} %copy-done.232, bf16[128,2560]{1,0:T(8,128)(2,1)} %copy-done.231, bf16[128,2560]{1,0:T(8,128)(2,1)} %copy-done.230, bf16[128,2560]{1,0:T(8,128)(2,1)} %copy-done.229, bf16[128,2560]{1,0:T(8,128)(2,1)S(1)} %copy-done.228, ...), kind=kOutput, calls=%fused_computation.297 | convolution fusion | flops 8091860992 | bytes 26476544 | tf_op jit(solution)/shard_map/dot_general | solution.py:76
  1107.7 45.1 %convert_element_type.590 = bf16[2048,2,2560]{2,1,0:T(2,128)(2,1)} reshape(bf16[2048,5120]{1,0:T(8,128)(2,1)} %convolution_convert_fusion.15) | data formatting | bytes 41943040 | tf_op jit(solution)/shard_map/convert_element_type | solution.py:496
  1159.5 8.3 convolution_convert_fusion.16
  1182.0 6.7 reduce-scatter.54.cloned.1.call-done
  1190.6 45.4 %reduce-scatter.50.cloned.1.call-done = bf16[256,640]{1,0:T(8,128)(2,1)} async-done(((bf16[2048,640]{1,0:T(8,128)(2,1)}), bf16[256,640]{1,0:T(8,128)(2,1)}) %reduce-scatter.50.cloned.1.call-update) | async-done | bytes 327696 | tf_op jit(solution)/shard_map/reduce_scatter | solution.py:488
  1237.8 15.1 reduce-scatter.48.cloned.1.call-done
  1256.0 53.6 %all-reduce.2 = f32[4224]{0:T(1024)S(1)} all-reduce(f32[4224]{0:T(1024)S(1)} %add_add_fusion), channel_id=28, replica_groups=mesh['section'=2,'tensor'=2,'ctx'=8] {'tensor','ctx'}, use_global_device_ids=true, to_apply=%region_89.90.clone | all-reduce | flops 4224 | bytes 33792
  1313.6 207.0 %all-reduce.5.cloned.1.call-done = bf16[2048,2,2560]{2,1,0:T(2,128)(2,1)} async-done(((bf16[2048,2,2560]{2,1,0:T(2,128)(2,1)}), bf16[2048,2,2560]{2,1,0:T(2,128)(2,1)}) %all-reduce.5.cloned.1.call-update) | async-done | bytes 20971536
  1520.6 5.9 bitcast_convert_fusion
  1526.5 79.1 %reduce-scatter.56.cloned.1.call-done = bf16[2560,256]{1,0:T(8,128)(2,1)} async-done(((bf16[2560,2048]{1,0:T(8,128)(2,1)}), bf16[2560,256]{1,0:T(8,128)(2,1)}) %reduce-scatter.56.cloned.1.call-update) | async-done | bytes 1310736 | tf_op jit(solution)/shard_map/reduce_scatter | solution.py:501
  1608.6 64.4 %reduce-scatter.52.cloned.1.call-done = f32[128,640]{1,0:T(8,128)} async-done(((f32[2048,640]{1,0:T(8,128)}), f32[128,640]{1,0:T(8,128)}) %reduce-scatter.52.cloned.1.call-update) | async-done | bytes 327696 | tf_op jit(solution)/shard_map/reduce_scatter | solution.py:491
  (1058 shorter events, 413.3 us)
Async XLA Ops:
  7.2 67.7 %all-gather.21.cloned.1.call-start = ((), (), s32[]{:S(2)}) async-start(), calls=%async_computation.38 | async-start | bytes 2785280 | tf_op jit(solution)/shard_map/all_gather | solution.py:297
  7.9 81.2 %all-gather.23.cloned.1.call-start = ((), (), s32[]{:S(2)}) async-start(), calls=%async_computation.39 | async-start | bytes 2949120 | tf_op jit(solution)/shard_map/all_gather | solution.py:293
  8.6 99.9 %all-gather.15.cloned.1.call-start = ((), (), s32[]{:S(2)}) async-start(), calls=%async_computation.19 | async-start | bytes 1392640 | tf_op jit(solution)/shard_map/all_gather | solution.py:361
  10.2 77.0 %copy-start.190 = (s32[8]{0:T(128)}, s32[8]{0:T(128)S(1)}, u32[]{:S(2)}) copy-start(s32[8]{0:T(128)S(1)} %get-tuple-element.1572) | copy-start | bytes 100
  10.2 77.1 %copy-start.192 = (s32[8]{0:T(128)}, s32[8]{0:T(128)S(1)}, u32[]{:S(2)}) copy-start(s32[8]{0:T(128)S(1)} %get-tuple-element.1586) | copy-start | bytes 100
  12.1 74.9 %copy-start.194 = (s32[8]{0:T(128)}, s32[8]{0:T(128)S(1)}, u32[]{:S(2)}) copy-start(s32[8]{0:T(128)S(1)} %get-tuple-element.1580) | copy-start | bytes 100
  73.7 293.9 %copy-start.101 = (f32[1,2048]{1,0:T(1,128)}, f32[1,2048]{1,0:T(1,128)S(1)}, u32[]{:S(2)}) copy-start(f32[1,2048]{1,0:T(1,128)S(1)} %get-tuple-element.1489) | copy-start | bytes 24580
  79.1 60.9 %all-gather.25.cloned.1.call-start = ((), (), s32[]{:S(2)}) async-start(), calls=%async_computation.40 | async-start | bytes 2949120 | tf_op jit(solution)/shard_map/all_gather | solution.py:294
  79.7 78.2 %reduce-scatter.26.cloned.1.call-start = ((), (), s32[]{:S(2)}) async-start(), calls=%async_computation.20 | async-start | bytes 786432 | tf_op jit(solution)/shard_map/reduce_scatter | solution.py:133
  143.2 124.2 %all-gather.27.cloned.1.call-start = ((), (), s32[]{:S(2)}) async-start(), calls=%async_computation.41 | async-start | bytes 23592960 | tf_op jit(solution)/shard_map/all_gather | solution.py:295
  143.8 190.9 %all-gather.29.cloned.1.call-start = ((), (), s32[]{:S(2)}) async-start(), calls=%async_computation.42 | async-start | bytes 11796480 | tf_op jit(solution)/shard_map/all_gather | solution.py:296
  144.5 211.3 %reduce-scatter.28.cloned.1.call-start = ((), (), s32[]{:S(2)}) async-start(), calls=%async_computation.21 | async-start | bytes 786432 | tf_op jit(solution)/shard_map/reduce_scatter | solution.py:133
  291.9 42.8 %copy-start.13 = (f32[128,5120]{1,0:T(8,128)}, f32[128,5120]{1,0:T(8,128)S(1)}, u32[]{:S(2)}) copy-start(f32[128,5120]{1,0:T(8,128)S(1)} %fusion.579) | copy-start | bytes 7864324
  291.9 64.0 %copy-start.66 = (bf16[64,2048]{1,0:T(8,128)(2,1)S(1)}, bf16[64,2048]{1,0:T(8,128)(2,1)}, u32[]{:S(2)}) copy-start(bf16[64,2048]{1,0:T(8,128)(2,1)} %reduce-scatter.26.cloned.1.call-done) | copy-start | bytes 786436
  341.1 28.1 %copy-start.1 = (bf16[1,2048,640]{2,1,0:T(8,128)(2,1)S(1)}, bf16[1,2048,640]{2,1,0:T(8,128)(2,1)}, u32[]{:S(2)}) copy-start(bf16[1,2048,640]{2,1,0:T(8,128)(2,1)} %all-gather.21.cloned.1.call-done) | copy-start | bytes 7864324
  341.1 72.1 %all-gather.17.cloned.1.call-start = ((), (), s32[]{:S(2)}) async-start(), calls=%async_computation.22 | async-start | bytes 1392640 | tf_op jit(solution)/shard_map/all_gather | solution.py:361
  357.0 9.9 collective-permute-start
  376.3 89.9 %reduce-scatter.30.cloned.1.call-start = ((), (), s32[]{:S(2)}) async-start(), calls=%async_computation.23 | async-start | bytes 786432 | tf_op jit(solution)/shard_map/reduce_scatter | solution.py:133
  393.2 26.9 %copy-start.127 = (f32[128,10]{0,1:T(8,128)}, f32[128,10]{0,1:T(8,128)S(1)}, u32[]{:S(2)}) copy-start(f32[128,10]{0,1:T(8,128)S(1)} %get-tuple-element.1498) | copy-start | bytes 15364
  452.4 53.8 %reduce-scatter.32.cloned.1.call-start = ((), (), s32[]{:S(2)}) async-start(), calls=%async_computation.24 | async-start | bytes 786432 | tf_op jit(solution)/shard_map/reduce_scatter | solution.py:133
  489.0 24.0 %copy-start.191 = (s32[8]{0:T(128)S(1)}, s32[8]{0:T(128)}, u32[]{:S(2)}) copy-start(s32[8]{0:T(128)} %copy-done.190) | copy-start | bytes 100
  489.0 24.0 %copy-start.193 = (s32[8]{0:T(128)S(1)}, s32[8]{0:T(128)}, u32[]{:S(2)}) copy-start(s32[8]{0:T(128)} %copy-done.192) | copy-start | bytes 100
  489.0 24.0 %copy-start.195 = (s32[8]{0:T(128)S(1)}, s32[8]{0:T(128)}, u32[]{:S(2)}) copy-start(s32[8]{0:T(128)} %copy-done.194) | copy-start | bytes 100
  491.5 71.6 %all-gather.19.cloned.1.call-start = ((), (), s32[]{:S(2)}) async-start(), calls=%async_computation.25 | async-start | bytes 1392640 | tf_op jit(solution)/shard_map/all_gather | solution.py:361
  508.0 10.2 collective-permute-start.1
  518.4 90.9 %copy-start.27 = (bf16[64,2048]{1,0:T(8,128)(2,1)}, bf16[64,2048]{1,0:T(8,128)(2,1)S(1)}, u32[]{:S(2)}) copy-start(bf16[64,2048]{1,0:T(8,128)(2,1)S(1)} %get-tuple-element.1379) | copy-start | bytes 786436
  521.2 31.1 %copy-start.5 = (bf16[1,2048,640]{2,1,0:T(8,128)(2,1)S(1)}, bf16[1,2048,640]{2,1,0:T(8,128)(2,1)}, u32[]{:S(2)}) copy-start(bf16[1,2048,640]{2,1,0:T(8,128)(2,1)} %all-gather.23.cloned.1.call-done) | copy-start | bytes 7864324
  524.4 83.7 %reduce-scatter.34.cloned.1.call-start = ((), (), s32[]{:S(2)}) async-start(), calls=%async_computation.26 | async-start | bytes 786432 | tf_op jit(solution)/shard_map/reduce_scatter | solution.py:133
  529.4 24.8 %copy-start.159 = (f32[64]{0:T(128)S(1)}, f32[64]{0:T(128)}, u32[]{:S(2)}) copy-start(f32[64]{0:T(128)} %copy-done.158) | copy-start | bytes 772
  594.1 78.8 %reduce-scatter.38.cloned.1.call-start = ((), (), s32[]{:S(2)}) async-start(), calls=%async_computation.28 | async-start | bytes 786432 | tf_op jit(solution)/shard_map/reduce_scatter | solution.py:133
  654.0 117.6 %reduce-scatter.58.cloned.1.call-start = ((), (), s32[]{:S(2)}) async-start(), calls=%async_computation.43 | async-start | bytes 2785280
  711.7 75.4 %reduce-scatter.40.cloned.1.call-start = ((), (), s32[]{:S(2)}) async-start(), calls=%async_computation.29 | async-start | bytes 786432 | tf_op jit(solution)/shard_map/reduce_scatter | solution.py:133
  725.7 48.6 %copy-start.144 = (f32[64,32]{0,1:T(8,128)S(1)}, f32[64,32]{0,1:T(8,128)}, u32[]{:S(2)}) copy-start(f32[64,32]{0,1:T(8,128)} %get-tuple-element.1475) | copy-start | bytes 24580
  725.7 50.3 %copy-start.166 = (f32[64]{0:T(128)S(1)}, f32[64]{0:T(128)}, u32[]{:S(2)}) copy-start(f32[64]{0:T(128)} %copy-done.163) | copy-start | bytes 772
  725.7 50.4 %copy-start.162 = (f32[320]{0:T(512)S(1)}, f32[320]{0:T(512)}, u32[]{:S(2)}) copy-start(f32[320]{0:T(512)} %mul.1754) | copy-start | bytes 3844
  725.7 125.3 %reduce-scatter.42.cloned.1.call-start = ((), (), s32[]{:S(2)}) async-start(), calls=%async_computation.30 | async-start | bytes 786432 | tf_op jit(solution)/shard_map/reduce_scatter | solution.py:133
  726.0 61.2 %copy-start.2 = (bf16[1,2048,640]{2,1,0:T(8,128)(2,1)S(1)}, bf16[1,2048,640]{2,1,0:T(8,128)(2,1)}, u32[]{:S(2)}) copy-start(bf16[1,2048,640]{2,1,0:T(8,128)(2,1)} %all-gather.21.cloned.1.call-done) | copy-start | bytes 7864324
  789.9 27.1 %copy-start.58 = (f32[128,5120]{1,0:T(8,128)S(1)}, f32[128,5120]{1,0:T(8,128)}, u32[]{:S(2)}) copy-start(f32[128,5120]{1,0:T(8,128)} %get-tuple-element.1389) | copy-start | bytes 7864324
  791.7 33.3 %copy-start.94 = (bf16[64,2048]{1,0:T(8,128)(2,1)}, bf16[64,2048]{1,0:T(8,128)(2,1)S(1)}, u32[]{:S(2)}) copy-start(bf16[64,2048]{1,0:T(8,128)(2,1)S(1)} %fusion.442) | copy-start | bytes 786436
  791.7 16.3 collective-permute-start.2
  838.1 110.2 %reduce-scatter.60.cloned.1.call-start = ((), (), s32[]{:S(2)}) async-start(), calls=%async_computation.44 | async-start | bytes 2785280
  888.6 75.5 %reduce-scatter.44.cloned.1.call-start = ((), (), s32[]{:S(2)}) async-start(), calls=%async_computation.31 | async-start | bytes 786432 | tf_op jit(solution)/shard_map/reduce_scatter | solution.py:133
  891.2 59.8 %copy-start.138 = (f32[64,32]{0,1:T(8,128)S(1)}, f32[64,32]{0,1:T(8,128)}, u32[]{:S(2)}) copy-start(f32[64,32]{0,1:T(8,128)} %get-tuple-element.1471) | copy-start | bytes 24580
  891.3 59.8 %copy-start.139 = (f32[64,32]{0,1:T(8,128)S(1)}, f32[64,32]{0,1:T(8,128)}, u32[]{:S(2)}) copy-start(f32[64,32]{0,1:T(8,128)} %get-tuple-element.1474) | copy-start | bytes 24580
  891.4 59.7 %copy-start.112 = (bf16[128,640]{0,1:T(8,128)(2,1)}, bf16[128,640]{0,1:T(8,128)(2,1)S(1)}, u32[]{:S(2)}) copy-start(bf16[128,640]{0,1:T(8,128)(2,1)S(1)} %fusion.483) | copy-start | bytes 491524
  891.5 60.8 %copy-start.167 = (f32[64]{0:T(128)S(1)}, f32[64]{0:T(128)}, u32[]{:S(2)}) copy-start(f32[64]{0:T(128)} %copy-done.163) | copy-start | bytes 772
  891.5 60.9 %copy-start.182 = (f32[64,5]{0,1:T(8,128)S(1)}, f32[64,5]{0,1:T(8,128)}, u32[]{:S(2)}) copy-start(f32[64,5]{0,1:T(8,128)} %get-tuple-element.1493) | copy-start | bytes 3844
  891.5 72.6 %copy-start.3 = (bf16[1,2048,640]{2,1,0:T(8,128)(2,1)S(1)}, bf16[1,2048,640]{2,1,0:T(8,128)(2,1)}, u32[]{:S(2)}) copy-start(bf16[1,2048,640]{2,1,0:T(8,128)(2,1)} %all-gather.21.cloned.1.call-done) | copy-start | bytes 7864324
  893.3 134.6 %reduce-scatter.46.cloned.1.call-start = ((), (), s32[]{:S(2)}) async-start(), calls=%async_computation.32 | async-start | bytes 786432 | tf_op jit(solution)/shard_map/reduce_scatter | solution.py:133
  966.4 27.6 %copy-start.57 = (f32[128,5120]{1,0:T(8,128)S(1)}, f32[128,5120]{1,0:T(8,128)}, u32[]{:S(2)}) copy-start(f32[128,5120]{1,0:T(8,128)} %get-tuple-element.1388) | copy-start | bytes 7864324
  968.2 33.7 %copy-start.100 = (bf16[64,2048]{1,0:T(8,128)(2,1)}, bf16[64,2048]{1,0:T(8,128)(2,1)S(1)}, u32[]{:S(2)}) copy-start(bf16[64,2048]{1,0:T(8,128)(2,1)S(1)} %fusion.436) | copy-start | bytes 786436
  968.2 16.3 collective-permute-start.3
  1014.9 154.1 %reduce-scatter.62.cloned.1.call-start = ((), (), s32[]{:S(2)}) async-start(), calls=%async_computation.45 | async-start | bytes 2785280
  1065.8 112.8 %reduce-scatter.36.cloned.1.call-start = ((), (), s32[]{:S(2)}) async-start(), calls=%async_computation.27 | async-start | bytes 786432 | tf_op jit(solution)/shard_map/reduce_scatter | solution.py:133
  1073.9 114.8 %reduce-scatter.54.cloned.1.call-start = ((), (), s32[]{:S(2)}) async-start(), calls=%async_computation.36 | async-start | bytes 2949120 | tf_op jit(solution)/shard_map/reduce_scatter | solution.py:492
  1078.6 157.4 %reduce-scatter.50.cloned.1.call-start = ((), (), s32[]{:S(2)}) async-start(), calls=%async_computation.34 | async-start | bytes 2949120 | tf_op jit(solution)/shard_map/reduce_scatter | solution.py:488
  1085.7 167.3 %reduce-scatter.48.cloned.1.call-start = ((), (), s32[]{:S(2)}) async-start(), calls=%async_computation.33 | async-start | bytes 786432 | tf_op jit(solution)/shard_map/reduce_scatter | solution.py:133
  1090.6 430.0 %all-reduce.5.cloned.1.call-start = ((), (), s32[]{:S(2)}) async-start(), calls=%async_computation.46 | async-start | bytes 41943040
  1152.8 452.8 %reduce-scatter.56.cloned.1.call-start = ((), (), s32[]{:S(2)}) async-start(), calls=%async_computation.37 | async-start | bytes 11796480 | tf_op jit(solution)/shard_map/reduce_scatter | solution.py:501
  1167.8 505.2 %reduce-scatter.52.cloned.1.call-start = ((), (), s32[]{:S(2)}) async-start(), calls=%async_computation.35 | async-start | bytes 5570560 | tf_op jit(solution)/shard_map/reduce_scatter | solution.py:491
  1179.8 73.1 %copy-start.4 = (bf16[1,2048,640]{2,1,0:T(8,128)(2,1)S(1)}, bf16[1,2048,640]{2,1,0:T(8,128)(2,1)}, u32[]{:S(2)}) copy-start(bf16[1,2048,640]{2,1,0:T(8,128)(2,1)} %all-gather.21.cloned.1.call-done) | copy-start | bytes 7864324
  1190.6 119.7 %copy-start.74 = (f32[64,2048]{1,0:T(8,128)S(1)}, f32[64,2048]{1,0:T(8,128)}, u32[]{:S(2)}) copy-start(f32[64,2048]{1,0:T(8,128)} %get-tuple-element.1377) | copy-start | bytes 1572868
  1190.6 119.7 %copy-start.220 = (f32[64]{0:T(128)S(1)}, f32[64]{0:T(128)}, u32[]{:S(2)}) copy-start(f32[64]{0:T(128)} %get-tuple-element.1513) | copy-start | bytes 772
  1237.8 73.9 %copy-start.95 = (bf16[64,2048]{1,0:T(8,128)(2,1)S(1)}, bf16[64,2048]{1,0:T(8,128)(2,1)}, u32[]{:S(2)}) copy-start(bf16[64,2048]{1,0:T(8,128)(2,1)} %copy-done.94) | copy-start | bytes 786436
  (205 other events, 1248.8 us)
Sparse Core Ops, SparseCore 0:
  9.6 35.1 all-gather.20
  46.6 29.4 all-gather.22
  79.2 29.3 all-gather.14
  110.3 29.6 all-gather.24
  143.3 14.5 reduce-scatter.25
  159.8 107.5 all-gather.26
  269.4 65.2 all-gather.28
  341.3 14.5 reduce-scatter.27
  376.4 36.7 all-gather.16
  452.5 13.6 reduce-scatter.29
  491.6 14.5 reduce-scatter.31
  524.6 38.4 all-gather.18
  594.2 13.8 reduce-scatter.33
  654.1 14.5 reduce-scatter.37
  711.8 59.7 reduce-scatter.57
  774.2 12.8 reduce-scatter.39
  838.2 12.8 reduce-scatter.41
  888.7 59.5 reduce-scatter.59
  951.1 12.8 reduce-scatter.43
  1015.1 12.7 reduce-scatter.45
  1065.9 59.6 reduce-scatter.61
  1128.5 12.7 reduce-scatter.35
  1145.0 43.6 reduce-scatter.53
  1192.3 43.6 reduce-scatter.49
  1238.3 14.5 reduce-scatter.47
  1256.5 264.0 all-reduce.4
  1524.0 81.5 reduce-scatter.55
  1608.4 64.5 reduce-scatter.51
where the time goes:
time: 1690 us; the launch traced here: 1680 us
  waiting for transfers between devices  846 us (50%)
  matrix products  253 us (15%)
  blocking collectives  223 us (13%)
  local copies, waits for them, and re-layouts  203 us (12%)
  other arithmetic  120 us (7%)
  between operations  21.9 us (1%)
    unnamed x32, waiting for transfers between devices  308 us
    all_gather x12, blocking collectives, gather_rows(): return lax.all_gather(values, 'tensor', axis=0, tiled=True)  114 us
    reduce_scatter x12, waiting for transfers between devices, scatter_rows(): lax.psum_scatter(values.astype(jnp.bfloat16), 'tensor', scatter_dimension...  113 us
    unnamed x2, blocking collectives  109 us
    all_gather x1, waiting for transfers between devices, per_device(): gateup_full = lax.all_gather(gateup_weight[0], 'ctx', axis=0, tiled=True)  96.9 us
    reduce_scatter x1, waiting for transfers between devices, per_device(): lax.psum_scatter(full_set[3].astype(jnp.bfloat16), 'ctx', scatter_dimensi...  79.1 us
    unnamed x488, local copies, waits for them, and re-layouts  69.7 us
    reduce_scatter x1, waiting for transfers between devices, per_device(): lax.psum_scatter(full_set[4], ('tensor', 'ctx'), scatter_dimension=0, til...  64.4 us
  transfers between devices with their start and end apart: 32, of which 27 were waited for; matrix products, arithmetic and copies ran while one was open for 16% of the time, Pallas kernels for 0%

commit v1 on v0

--- a/solution.py
+++ b/solution.py
@@ -1,6 +1,8 @@
 import jax
 import jax.numpy as jnp
 from jax import lax
+from jax.experimental import pallas as pl
+from jax.experimental.pallas import tpu as pltpu
 from jax.sharding import PartitionSpec as P
 
 MODEL_WIDTH = 2048
@@ -505,9 +507,1024 @@
     )
 
 
+C_BIT, X_BIT, Y_BIT, Z_BIT = 1, 2, 4, 8
+MESH_ID = pl.DeviceIdType.MESH
+ANY = pl.BlockSpec(memory_space=pl.ANY)
+VMEM = pl.BlockSpec(memory_space=pltpu.VMEM)
+SMEM = pl.BlockSpec(memory_space=pltpu.SMEM)
+F32 = jnp.float32
+BF16 = jnp.bfloat16
+GROUP = QUERY_HEADS // KEY_VALUE_HEADS
+KEY_COLUMNS = KEY_VALUE_HEADS * HEAD_SIZE
+QUERY_COLUMNS = QUERY_HEADS * HEAD_SIZE
+SCALE = HEAD_SIZE ** (-0.5)
+VMEM_BYTES = 60 * 2**20
+CYCLES = ((X_BIT, Y_BIT, Z_BIT), (Y_BIT, Z_BIT, X_BIT), (Z_BIT, X_BIT, Y_BIT))
+TOWARD_Z = ((X_BIT, Y_BIT, Z_BIT), (Y_BIT, X_BIT, Z_BIT))
+
+
+class Place:
+    def __init__(self):
+        self.section = lax.axis_index("section")
+        ctx = lax.axis_index("ctx")
+        self.bits = (ctx % 2, (ctx // 2) % 2, ctx // 4, lax.axis_index("tensor"))
+
+    def flipped(self, mask):
+        return [1 - bit if mask & (1 << i) else bit for i, bit in enumerate(self.bits)]
+
+    def block(self, mask=0):
+        core, x, y, z = self.flipped(mask)
+        return z * 8 + y * 4 + x * 2 + core
+
+    def ctx(self, mask=0):
+        core, x, y, z = self.flipped(mask)
+        return y * 4 + x * 2 + core
+
+    def peer(self, mask):
+        core, x, y, z = self.flipped(mask)
+        return (self.section, z, y * 4 + x * 2 + core)
+
+    def other_section(self, section):
+        core, x, y, z = self.bits
+        return (section, z, y * 4 + x * 2 + core)
+
+
+def remote(src, dst, send, recv, device):
+    return pltpu.make_async_remote_copy(
+        src_ref=src, dst_ref=dst, send_sem=send, recv_sem=recv, device_id=device, device_id_type=MESH_ID
+    )
+
+
+def greet(place, masks, into=None):
+    barrier = pltpu.get_barrier_semaphore()
+    for mask in masks:
+        pl.semaphore_signal(barrier, inc=1, device_id=place.peer(mask), device_id_type=MESH_ID)
+    if into is None:
+        pl.semaphore_wait(barrier, len(masks))
+        return
+
+    @pl.when(place.section == into)
+    def _():
+        pl.semaphore_signal(barrier, inc=1, device_id=place.other_section(1 - into), device_id_type=MESH_ID)
+        pl.semaphore_wait(barrier, len(masks))
+
+    @pl.when(place.section != into)
+    def _():
+        pl.semaphore_wait(barrier, len(masks) + 1)
+
+
+def column_pieces(widths, orders):
+    start, pieces = 0, []
+    for width, order in zip(widths, orders):
+        pieces.append(((slice(None), pl.ds(start, width)), order))
+        start += width
+    return pieces
+
+
+def row_pieces(heights, orders):
+    start, pieces = 0, []
+    for height, order in zip(heights, orders):
+        pieces.append(((pl.ds(start, height), slice(None)), order))
+        start += height
+    return pieces
+
+
+class Gather:
+    def __init__(self, place, buf, pieces, send, recv):
+        self.place, self.buf, self.pieces = place, buf, pieces
+        self.send, self.recv = send, recv
+        self.sent = []
+
+    def _copy(self, piece, mask, dim):
+        index = self.pieces[piece][0]
+        block = self.place.block(mask)
+        where = self.buf.at[(block,) + index]
+        slot = piece * 16 + (mask ^ dim)
+        return remote(where, where, self.send.at[slot], self.recv.at[slot], self.place.peer(dim))
+
+    def _start(self, piece, mask, dim):
+        copy = self._copy(piece, mask, dim)
+        copy.start()
+        self.sent.append(copy)
+
+    def _arrived(self, piece, mask, dim):
+        index = self.pieces[piece][0]
+        where = self.buf.at[(self.place.block(mask),) + index]
+        slot = piece * 16 + mask
+        remote(where, where, self.send.at[slot], self.recv.at[slot], self.place.peer(dim)).wait_recv()
+
+    def start(self):
+        for piece, (_, order) in enumerate(self.pieces):
+            for dim in order:
+                self._start(piece, 0, dim)
+        for piece in range(len(self.pieces)):
+            self._start(piece, 0, C_BIT)
+
+    def finish(self):
+        pieces = list(enumerate(self.pieces))
+        for piece, (_, (d0, d1, d2)) in pieces:
+            self._arrived(piece, d0, d0)
+            self._start(piece, d0, d1)
+            self._start(piece, d0, d2)
+            self._start(piece, d0, C_BIT)
+        for piece, (_, (d0, d1, d2)) in pieces:
+            self._arrived(piece, d1, d1)
+            self._start(piece, d1, d2)
+            self._start(piece, d1, C_BIT)
+        for piece, (_, (d0, d1, d2)) in pieces:
+            self._arrived(piece, d0 ^ d1, d1)
+            self._start(piece, d0 ^ d1, d2)
+            self._start(piece, d0 ^ d1, C_BIT)
+        for part in (0, 1, 2, 3):
+            for piece, (_, (d0, d1, d2)) in pieces:
+                mask = (d2, d0 ^ d2, d1 ^ d2, d0 ^ d1 ^ d2)[part]
+                self._arrived(piece, mask, d2)
+                self._start(piece, mask, C_BIT)
+        for piece, (_, (d0, d1, d2)) in pieces:
+            for mask in (0, d0, d1, d0 ^ d1, d2, d0 ^ d2, d1 ^ d2, d0 ^ d1 ^ d2):
+                self._arrived(piece, mask ^ C_BIT, C_BIT)
+        for copy in self.sent:
+            copy.wait_send()
+
+
+class Scatter:
+    MASKS = (14, 12, 10, 6, 8, 4, 2, 0)
+
+    def __init__(self, place, part, sib_recv, landed, pieces, send, recv, put):
+        self.place, self.part, self.pieces, self.put = place, part, pieces, put
+        self.sib_recv, self.landed = sib_recv, landed
+        self.send, self.recv = send, recv
+        self.sent = []
+
+    def _sib(self, i, mask):
+        slot = 3 * 16 + i
+        return remote(
+            self.part.at[self.place.block(mask | C_BIT)],
+            self.sib_recv.at[i],
+            self.send.at[slot],
+            self.recv.at[slot],
+            self.place.peer(C_BIT),
+        )
+
+    def start_sibling(self):
+        for i, mask in enumerate(self.MASKS):
+            copy = self._sib(i, mask)
+            copy.start()
+            self.sent.append(copy)
+
+    def add_sibling(self):
+        for i, mask in enumerate(self.MASKS):
+            self._sib(i, mask).wait_recv()
+            block = self.place.block(mask)
+            self.part[block] = (self.part[block].astype(F32) + self.sib_recv[i].astype(F32)).astype(BF16)
+
+    def _copy(self, piece, mask, dim):
+        index = self.pieces[piece][0]
+        slot = piece * 16 + mask
+        return remote(
+            self.part.at[(self.place.block(mask),) + index],
+            self.landed.at[(mask // 2,) + index],
+            self.send.at[slot],
+            self.recv.at[slot],
+            self.place.peer(dim),
+        )
+
+    def _start(self, piece, mask, dim):
+        copy = self._copy(piece, mask, dim)
+        copy.start()
+        self.sent.append(copy)
+
+    def _sum(self, piece, mask, dim):
+        self._copy(piece, mask, dim).wait_recv()
+        index = self.pieces[piece][0]
+        at = (self.place.block(mask ^ dim),) + index
+        return at, self.part[at].astype(F32) + self.landed[(mask // 2,) + index].astype(F32)
+
+    def _add(self, piece, mask, dim):
+        at, total = self._sum(piece, mask, dim)
+        self.part[at] = total.astype(BF16)
+
+    def finish(self):
+        pieces = list(enumerate(self.pieces))
+        for piece, (_, (d0, d1, d2)) in pieces:
+            for mask in (d0 ^ d1 ^ d2, d1 ^ d2):
+                self._start(piece, mask, d2)
+        for piece, (_, (d0, d1, d2)) in pieces:
+            for mask in (d0 ^ d2, d2):
+                self._start(piece, mask, d2)
+        for piece, (_, (d0, d1, d2)) in pieces:
+            for mask in (d0 ^ d1, d1):
+                self._add(piece, mask ^ d2, d2)
+                self._start(piece, mask, d1)
+        for piece, (_, (d0, d1, d2)) in pieces:
+            for mask in (d0, 0):
+                self._add(piece, mask ^ d2, d2)
+        for piece, (_, (d0, d1, d2)) in pieces:
+            self._add(piece, d0 ^ d1, d1)
+            self._start(piece, d0, d0)
+        for piece, (_, (d0, d1, d2)) in pieces:
+            self._add(piece, d1, d1)
+        for piece, (index, (d0, d1, d2)) in pieces:
+            _, total = self._sum(piece, d0, d0)
+            self.put(index, total)
+
+    def drain(self):
+        for copy in self.sent:
+            copy.wait_send()
+
+
+def gather_sems(pieces):
+    return [pltpu.SemaphoreType.DMA((16 * pieces,)), pltpu.SemaphoreType.DMA((16 * pieces,))]
+
+
+def scatter_sems():
+    return [pltpu.SemaphoreType.DMA((64,)), pltpu.SemaphoreType.DMA((64,))]
+
+
+def kernel_params(collective):
+    return pltpu.CompilerParams(collective_id=collective, has_side_effects=True, vmem_limit_bytes=VMEM_BYTES)
+
+
+def weights_kernel(q_ref, kv_ref, o_ref, gu_ref, dn_ref, g_ref, q_all, kv_all, o_all, gu_mine, dn_mine, g_all,
+                   q_send, q_recv, kv_send, kv_recv, o_send, o_recv, g_send, g_recv, a_send, a_recv, local):
+    place = Place()
+    own = place.block()
+    ctx = place.ctx()
+    units = dn_mine.shape[0]
+    width = dn_ref.shape[1]
+    others = (1, 2, 3, 4, 5, 6, 7)
+    greet(place, others + (Z_BIT,))
+    locals_ = []
+    for i, (src, dst) in enumerate(((q_ref, q_all), (kv_ref, kv_all), (o_ref, o_all), (g_ref, g_all))):
+        copy = pltpu.make_async_copy(src, dst.at[own], local.at[i])
+        copy.start()
+        locals_.append(copy)
+    for copy in locals_:
+        copy.wait()
+    gathers = []
+    for buf, send, recv in ((q_all, q_send, q_recv), (kv_all, kv_send, kv_recv), (o_all, o_send, o_recv)):
+        half = buf.shape[1] // 2
+        gathers.append(Gather(place, buf, row_pieces((half, half), TOWARD_Z), send, recv))
+    gathers.append(Gather(place, g_all, row_pieces((g_ref.shape[0],), TOWARD_Z), g_send, g_recv))
+    for gather in gathers:
+        gather.start()
+
+    def shares(mask, back=0):
+        there = place.ctx(mask)
+        rows = pl.ds(pl.multiple_of(there * units, 16), units)
+        columns = pl.ds(pl.multiple_of((place.ctx(mask) if back else ctx) * width, 128), width)
+        return (gu_ref.at[:, rows, :], gu_mine.at[:, :, columns]), (dn_ref.at[rows, :], dn_mine.at[:, columns])
+
+    sent = []
+    for mask in (6, 7, 2, 3, 4, 5, 1):
+        for j, (src, dst) in enumerate(shares(mask)):
+            slot = 2 * mask + j
+            copy = remote(src, dst, a_send.at[slot], a_recv.at[slot], place.peer(mask))
+            copy.start()
+            sent.append(copy)
+    kept = []
+    for j, (src, dst) in enumerate(shares(0)):
+        copy = pltpu.make_async_copy(src, dst, local.at[4 + j])
+        copy.start()
+        kept.append(copy)
+    for gather in gathers:
+        gather.finish()
+    for copy in kept:
+        copy.wait()
+    for mask in others:
+        for j, (src, dst) in enumerate(shares(mask, 1)):
+            slot = 2 * mask + j
+            remote(src, dst, a_send.at[slot], a_recv.at[slot], place.peer(mask)).wait_recv()
+    for copy in sent:
+        copy.wait_send()
+
+
+def bring_weights(query, keyval, out, gateup, down, gains):
+    units = down.shape[0] // 8
+    width = gateup.shape[2] * 8
+    shape = jax.ShapeDtypeStruct
+    return pl.pallas_call(
+        weights_kernel,
+        out_shape=(
+            shape((16,) + query.shape, BF16),
+            shape((16,) + keyval.shape, BF16),
+            shape((16,) + out.shape, BF16),
+            shape((2, units, width), BF16),
+            shape((units, width), BF16),
+            shape((16,) + gains.shape, BF16),
+        ),
+        in_specs=[ANY] * 6,
+        out_specs=[ANY] * 6,
+        scratch_shapes=gather_sems(2) * 3
+        + gather_sems(1)
+        + [pltpu.SemaphoreType.DMA((16,)), pltpu.SemaphoreType.DMA((16,)), pltpu.SemaphoreType.DMA((6,))],
+        compiler_params=kernel_params(0),
+    )(query, keyval, out, gateup, down, gains)
+
+
+def dot(left, right):
+    return lax.dot_general(left, right, (((1,), (0,)), ((), ())), preferred_element_type=F32)
+
+
+def dot_nt(left, right):
+    return lax.dot_general(left, right, (((1,), (1,)), ((), ())), preferred_element_type=F32)
+
+
+def dot_tn(left, right):
+    return lax.dot_general(left, right, (((0,), (0,)), ((), ())), preferred_element_type=F32)
+
+
+def unit_rows(values):
+    inverse = lax.rsqrt(jnp.mean(values * values, axis=-1, keepdims=True) + EPSILON)
+    return values * inverse, inverse
+
+
+def unit_back(scaled, unit, inverse):
+    return inverse * (scaled - unit * jnp.mean(scaled * unit, axis=-1, keepdims=True))
+
+
+def stack_heads(values, heads):
+    return jnp.concatenate([values[:, h * HEAD_SIZE : (h + 1) * HEAD_SIZE] for h in range(heads)], axis=0)
+
+
+def spread_heads(values, heads):
+    rows = values.shape[0] // heads
+    return jnp.concatenate([values[h * rows : (h + 1) * rows] for h in range(heads)], axis=1)
+
+
+def turned(values):
+    half = HEAD_SIZE // 2
+    return jnp.concatenate([values[:, half:], values[:, :half]], axis=1)
+
+
+def tall(rows, times):
+    return jnp.concatenate([rows] * times, axis=0)
+
+
+def rope(values, cos, sin, heads):
+    return values * tall(cos, heads) + turned(values) * tall(sin, heads)
+
+
+def unrope(values, cos, sin, heads):
+    return values * tall(cos, heads) - turned(values) * tall(sin, heads)
+
+
+def low32(values):
+    return values.astype(BF16).astype(F32)
+
+
+def attention_inputs(m, rowtab, postab, bias):
+    allowed = postab[m, 0:1, :] <= rowtab[m, :, 128:129]
+    bias[...] = jnp.where(allowed, 0.0, -jnp.inf)
+
+
+def split_keys(kv, k5, v5):
+    rows = kv.shape[0] * kv.shape[1]
+    for g in range(KEY_VALUE_HEADS):
+        k5[g] = kv[:, :, g * HEAD_SIZE : (g + 1) * HEAD_SIZE].reshape(rows, HEAD_SIZE)
+        v5[g] = kv[:, :, KEY_COLUMNS + g * HEAD_SIZE : KEY_COLUMNS + (g + 1) * HEAD_SIZE].reshape(rows, HEAD_SIZE)
+
+
+def probabilities(queries, keys, bias):
+    scores = dot_nt(queries, keys) + tall(bias, GROUP)
+    raised = jnp.exp(scores - jnp.max(scores, axis=-1, keepdims=True))
+    return raised / jnp.sum(raised, axis=-1, keepdims=True)
+
+
+E_WIDTHS = (768, 640, 640)
+KV_WIDTHS = (256, 256, 128)
+CHUNK = 256
+
+
+def load(src, dst, sem):
+    copy = pltpu.make_async_copy(src, dst, sem)
+    copy.start()
+    return copy
+
+
+def forward_kernel(m_ref, inputs_ref, received_ref, rowtab, postab, gains, q_hbm, kv_hbm, o_hbm, gu_hbm, dn_hbm,
+                   result_ref, passed_ref, u_ref, h_ref, qraw_ref, kraw_ref, qrot_ref, kvall_hbm, ob_ref, e_hbm, gu_t_hbm,
+                   hid_hbm,
+                   wq, wkv, wo, wgu, wdn, kv, e, gu_t, hid, k5, v5, o5, bias, part, sib_recv, landed,
+                   kv_send, kv_recv, e_send, e_recv, y_send, y_recv, pass_send, pass_recv, local):
+    place = Place()
+    own = place.block()
+    loads = [
+        load(src, dst, local.at[i])
+        for i, (src, dst) in enumerate(((kv_hbm, wkv), (q_hbm, wq), (o_hbm, wo), (gu_hbm, wgu), (dn_hbm, wdn)))
+    ]
+    greet(place, (C_BIT, X_BIT, Y_BIT, Z_BIT), into=1)
+    m = m_ref[0]
+    rows = u_ref.shape[0]
+    width = u_ref.shape[1]
+    attn_gain, ffn_gain = gains[:, :width], gains[:, width : 2 * width]
+    q_gain = gains[:, 2 * width : 2 * width + HEAD_SIZE]
+    k_gain = gains[:, 2 * width + HEAD_SIZE : 2 * width + 2 * HEAD_SIZE]
+    cos, sin = rowtab[m, :, :HEAD_SIZE], rowtab[m, :, HEAD_SIZE : 2 * HEAD_SIZE]
+
+    u_low = jnp.where(place.section == 0, inputs_ref[m], received_ref[...])
+    u_ref[...] = u_low
+    u = u_low.astype(F32)
+    a = (unit_rows(u)[0] * attn_gain).astype(BF16)
+
+    loads[0].wait()
+    kv_raw = dot(a, wkv[...].reshape(width, 2 * KEY_COLUMNS))
+    k_raw = stack_heads(kv_raw[:, :KEY_COLUMNS], KEY_VALUE_HEADS)
+    kraw_ref[...] = k_raw
+    k_low = rope(unit_rows(k_raw)[0] * k_gain, cos, sin, KEY_VALUE_HEADS).astype(BF16)
+    kv[own] = jnp.concatenate([spread_heads(k_low, KEY_VALUE_HEADS), kv_raw[:, KEY_COLUMNS:].astype(BF16)], axis=1)
+    kv_gather = Gather(place, kv, column_pieces(KV_WIDTHS, CYCLES), kv_send, kv_recv)
+    kv_gather.start()
+
+    loads[1].wait()
+    half = QUERY_COLUMNS // 2
+    q_raw = jnp.concatenate([dot(a, wq[t * 8 : t * 8 + 8].reshape(width, half)) for t in range(2)], axis=1)
+    q_raw = stack_heads(q_raw, QUERY_HEADS)
+    qraw_ref[...] = q_raw
+    q_low = (rope(unit_rows(q_raw)[0] * q_gain, cos, sin, QUERY_HEADS) * SCALE).astype(BF16)
+    qrot_ref[...] = q_low.reshape(KEY_VALUE_HEADS, GROUP * rows, HEAD_SIZE)
+    attention_inputs(m, rowtab, postab, bias)
+    kv_gather.finish()
+    saves = [load(kv, kvall_hbm, local.at[5])]
+    split_keys(kv, k5, v5)
+
+    def attend(g, _):
+        low = probabilities(qrot_ref[g], k5[g], bias[...]).astype(BF16)
+        o5[g] = dot(low, v5[g])
+        return 0
+
+    lax.fori_loop(0, KEY_VALUE_HEADS, attend, 0)
+    mixture = spread_heads(o5[...].reshape(QUERY_HEADS * rows, HEAD_SIZE), QUERY_HEADS).astype(BF16)
+    ob_ref[...] = mixture
+    loads[2].wait()
+    for c in range(8):
+        block = pl.ds(c * (width // 8), width // 8)
+        h_ref[:, block] = u_ref[:, block].astype(F32) + (
+            dot(ob_ref[:, :half], wo[c]) + dot(ob_ref[:, half:], wo[8 + c])
+        )
+    e[own] = (unit_rows(h_ref[...])[0] * ffn_gain).astype(BF16)
+    e_gather = Gather(place, e, column_pieces(E_WIDTHS, CYCLES), e_send, e_recv)
+    e_gather.start()
+    loads[3].wait()
+    loads[4].wait()
+    units = wdn.shape[0]
+    e_gather.finish()
+    saves.append(load(e, e_hbm, local.at[6]))
+
+    blocks = CHUNK // rows
+
+    def expand(i, _):
+        first = pl.multiple_of(i * blocks, blocks)
+        tokens = pl.ds(pl.multiple_of(i * CHUNK, CHUNK), CHUNK)
+        rows_here = e[pl.ds(first, blocks)].reshape(CHUNK, width)
+        both = dot_nt(wgu[...].reshape(2 * units, width), rows_here)
+        gu_t[:, tokens] = both
+        gate = both[:units]
+        hidden = (gate * jax.nn.sigmoid(gate) * both[units:]).astype(BF16)
+        hid[:, tokens] = hidden
+        part[pl.ds(first, blocks)] = dot_tn(hidden, wdn[...]).astype(BF16).reshape(blocks, rows, width)
+        return 0
+
+    lax.fori_loop(0, e.shape[0] // blocks, expand, 0)
+    saves.append(load(gu_t, gu_t_hbm, local.at[7]))
+    saves.append(load(hid, hid_hbm, local.at[8]))
+
+    def put(index, total):
+        result_ref[index] = (h_ref[index] + total).astype(BF16)
+
+    scatter = Scatter(place, part, sib_recv, landed, column_pieces(E_WIDTHS, CYCLES), y_send, y_recv, put)
+    scatter.start_sibling()
+    scatter.add_sibling()
+    scatter.finish()
+    onward = remote(result_ref, passed_ref, pass_send, pass_recv, place.other_section(1))
+
+    @pl.when(place.section == 0)
+    def _():
+        onward.start()
+        passed_ref[...] = jnp.zeros_like(passed_ref)
+        onward.wait_send()
+
+    @pl.when(place.section == 1)
+    def _():
+        onward.wait_recv()
+
+    scatter.drain()
+    for copy in saves:
+        copy.wait()
+
+
+def forward_step(m, inputs, received, rowtab, postab, gains, weights):
+    q_all, kv_all, o_all, gu_mine, dn_mine = weights
+    rows, width = received.shape
+    units = dn_mine.shape[0]
+    tokens = 16 * rows
+    shape = jax.ShapeDtypeStruct
+    return pl.pallas_call(
+        forward_kernel,
+        out_shape=(
+            shape((rows, width), BF16),
+            shape((rows, width), BF16),
+            shape((rows, width), BF16),
+            shape((rows, width), F32),
+            shape((QUERY_HEADS * rows, HEAD_SIZE), F32),
+            shape((KEY_VALUE_HEADS * rows, HEAD_SIZE), F32),
+            shape((KEY_VALUE_HEADS, GROUP * rows, HEAD_SIZE), BF16),
+            shape((16, rows, 2 * KEY_COLUMNS), BF16),
+            shape((rows, QUERY_COLUMNS), BF16),
+            shape((16, rows, width), BF16),
+            shape((2 * units, tokens), F32),
+            shape((units, tokens), BF16),
+        ),
+        in_specs=[SMEM] + [VMEM] * 5 + [ANY] * 5,
+        out_specs=[VMEM] * 7 + [ANY, VMEM, ANY, ANY, ANY],
+        scratch_shapes=[
+            pltpu.VMEM(q_all.shape, BF16),
+            pltpu.VMEM(kv_all.shape, BF16),
+            pltpu.VMEM(o_all.shape, BF16),
+            pltpu.VMEM(gu_mine.shape, BF16),
+            pltpu.VMEM(dn_mine.shape, BF16),
+            pltpu.VMEM((16, rows, 2 * KEY_COLUMNS), BF16),
+            pltpu.VMEM((16, rows, width), BF16),
+            pltpu.VMEM((2 * units, tokens), F32),
+            pltpu.VMEM((units, tokens), BF16),
+            pltpu.VMEM((KEY_VALUE_HEADS, tokens, HEAD_SIZE), BF16),
+            pltpu.VMEM((KEY_VALUE_HEADS, tokens, HEAD_SIZE), BF16),
+            pltpu.VMEM((KEY_VALUE_HEADS, GROUP * rows, HEAD_SIZE), F32),
+            pltpu.VMEM((rows, tokens), F32),
+            pltpu.VMEM((16, rows, width), BF16),
+            pltpu.VMEM((8, rows, width), BF16),
+            pltpu.VMEM((8, rows, width), BF16),
+        ]
+        + gather_sems(3)
+        + gather_sems(3)
+        + scatter_sems()
+        + [pltpu.SemaphoreType.DMA, pltpu.SemaphoreType.DMA, pltpu.SemaphoreType.DMA((9,))],
+        compiler_params=kernel_params(1),
+    )(m, inputs, received, rowtab, postab, gains, q_all, kv_all, o_all, gu_mine, dn_mine)
+
+
+def backward_kernel(m_ref, cot_ref, returned_ref, rowtab, postab, gains, q_hbm, kv_hbm, o_hbm, gu_hbm, dn_hbm,
+                    u_0, h_0, qraw_0, kraw_0, qrot_0, kvall_0, gu_t_0, u_1, h_1, qraw_1, kraw_1, qrot_1, kvall_1, gu_t_1,
+                    grad_ref, passed_ref, df_hbm, dgu_hbm, a_ref, da_ref, dq_ref, dkv_ref, gain_ref,
+                    wq, wkv, wo, wgu, wdn, u, h, qraw, kraw, qrot, kvall, gu_t, df, dgu, dh, dx, k5, v5, do5, dq5, dk5,
+                    dv5, bias, part, sib_recv, landed, part_kv, sib_recv_kv, landed_kv, dkv_own,
+                    df_send, df_recv, de_send, de_recv, kv_send, kv_recv, pass_send, pass_recv, local, state):
+    place = Place()
+    own = place.block()
+    kept = (u, h, qraw, kraw, qrot, kvall, gu_t)
+    for section, held in ((0, (u_0, h_0, qraw_0, kraw_0, qrot_0, kvall_0, gu_t_0)),
+                          (1, (u_1, h_1, qraw_1, kraw_1, qrot_1, kvall_1, gu_t_1))):
+
+        @pl.when(place.section == section)
+        def _(held=held):
+            for i, (src, dst) in enumerate(zip(held, kept)):
+                load(src, dst, state.at[i])
+
+    loads = [
+        load(src, dst, local.at[i])
+        for i, (src, dst) in enumerate(((dn_hbm, wdn), (gu_hbm, wgu), (o_hbm, wo), (q_hbm, wq), (kv_hbm, wkv)))
+    ]
+    greet(place, (C_BIT, X_BIT, Y_BIT, Z_BIT), into=0)
+    m = m_ref[0]
+    rows, width = u.shape
+    half = QUERY_COLUMNS // 2
+    attn_gain, ffn_gain = gains[:, :width], gains[:, width : 2 * width]
+    q_gain = gains[:, 2 * width : 2 * width + HEAD_SIZE]
+    k_gain = gains[:, 2 * width + HEAD_SIZE : 2 * width + 2 * HEAD_SIZE]
+    cos, sin = rowtab[m, :, :HEAD_SIZE], rowtab[m, :, HEAD_SIZE : 2 * HEAD_SIZE]
+
+    dy = jnp.where(place.section == 1, cot_ref[m], returned_ref[...])
+    df[own] = dy
+    dh[...] = dy.astype(F32)
+    df_gather = Gather(place, df, column_pieces(E_WIDTHS, CYCLES), df_send, df_recv)
+    df_gather.start()
+    for i, dst in enumerate(kept):
+        pltpu.make_async_copy(dst, dst, state.at[i]).wait()
+    attention_inputs(m, rowtab, postab, bias)
+    split_keys(kvall, k5, v5)
+    loads[0].wait()
+    loads[1].wait()
+    df_gather.finish()
+    saves = [load(df, df_hbm, local.at[5])]
+    units = wdn.shape[0]
+    blocks = CHUNK // rows
+
+    def shrink(i, _):
+        first = pl.multiple_of(i * blocks, blocks)
+        tokens = pl.ds(pl.multiple_of(i * CHUNK, CHUNK), CHUNK)
+        rows_here = df[pl.ds(first, blocks)].reshape(CHUNK, width)
+        dhidden = dot_nt(wdn[...], rows_here)
+        gate, up = gu_t[:units, tokens], gu_t[units:, tokens]
+        open_ = jax.nn.sigmoid(gate)
+        dgate = dhidden * up * (open_ * (1.0 + gate * (1.0 - open_)))
+        both = jnp.concatenate([dgate, dhidden * (gate * open_)], axis=0).astype(BF16)
+        dgu[:, tokens] = both
+        part[pl.ds(first, blocks)] = (
+            dot_tn(both, wgu[...].reshape(2 * units, width)).astype(BF16).reshape(blocks, rows, width)
+        )
+        return 0
+
+    lax.fori_loop(0, df.shape[0] // blocks, shrink, 0)
+    saves.append(load(dgu, dgu_hbm, local.at[6]))
+
+    def put(index, total):
+        dx[index] = total
+
+    scatter = Scatter(place, part, sib_recv, landed, column_pieces(E_WIDTHS, CYCLES), de_send, de_recv, put)
+    scatter.start_sibling()
+    scatter.add_sibling()
+    scatter.finish()
+    unit, inverse = unit_rows(h[...])
+    gain_ref[:, width : 2 * width] = jnp.sum(dx[...] * unit, axis=0, keepdims=True)
+    dh[...] = dh[...] + unit_back(dx[...] * ffn_gain, unit, inverse)
+    da_ref[...] = dh[...].astype(BF16)
+    loads[2].wait()
+    for t in range(2):
+        total = jnp.zeros((rows, half), F32)
+        for c in range(8):
+            total = total + dot_nt(da_ref[:, c * (width // 8) : (c + 1) * (width // 8)], wo[t * 8 + c])
+        heads = QUERY_HEADS // 2
+        stacked = stack_heads(total.astype(BF16), heads)
+        do5[t * heads * rows : (t + 1) * heads * rows] = stacked
+
+    def attend(g, _):
+        at = pl.ds(pl.multiple_of(g * GROUP * rows, GROUP * rows), GROUP * rows)
+        weights = probabilities(qrot[g], k5[g], bias[...])
+        grads = do5[at]
+        dweights = dot_nt(grads, v5[g])
+        inner = jnp.sum(weights * dweights, axis=-1, keepdims=True)
+        dscores = (weights * (dweights - inner)).astype(BF16)
+        dq5[at] = dot(dscores, k5[g])
+        dk5[g] = dot_tn(dscores, qrot[g])
+        dv5[g] = dot_tn(weights.astype(BF16), grads)
+        return 0
+
+    lax.fori_loop(0, KEY_VALUE_HEADS, attend, 0)
+    for b in range(16):
+        at = slice(b * rows, (b + 1) * rows)
+        part_kv[b] = jnp.concatenate(
+            [dk5[g, at] for g in range(KEY_VALUE_HEADS)] + [dv5[g, at] for g in range(KEY_VALUE_HEADS)], axis=1
+        ).astype(BF16)
+
+    def put_kv(index, total):
+        dkv_own[index] = total
+
+    scatter_kv = Scatter(
+        place, part_kv, sib_recv_kv, landed_kv, column_pieces(KV_WIDTHS, CYCLES), kv_send, kv_recv, put_kv
+    )
+    scatter_kv.start_sibling()
+    scatter_kv.add_sibling()
+
+    q_unit, q_inverse = unit_rows(qraw[...])
+    dqhat = unrope(dq5[...] * SCALE, cos, sin, QUERY_HEADS)
+    dq_gain = jnp.sum(dqhat * q_unit, axis=0, keepdims=True)
+    dq_raw = unit_back(dqhat * q_gain, q_unit, q_inverse)
+    dq_ref[...] = spread_heads(dq_raw, QUERY_HEADS).astype(BF16)
+    loads[3].wait()
+    loads[4].wait()
+    dx[...] = dot_nt(dq_ref[:, :half], wq[:8].reshape(width, half)) + dot_nt(dq_ref[:, half:], wq[8:].reshape(width, half))
+    scatter_kv.finish()
+
+    k_unit, k_inverse = unit_rows(kraw[...])
+    dkhat = unrope(stack_heads(dkv_own[:, :KEY_COLUMNS], KEY_VALUE_HEADS), cos, sin, KEY_VALUE_HEADS)
+    dk_gain = jnp.sum(dkhat * k_unit, axis=0, keepdims=True)
+    dk_raw = unit_back(dkhat * k_gain, k_unit, k_inverse)
+    gain_ref[:, 2 * width :] = jnp.concatenate([dq_gain, dk_gain], axis=1)
+    dkv_ref[...] = jnp.concatenate([spread_heads(dk_raw, KEY_VALUE_HEADS), dkv_own[:, KEY_COLUMNS:]], axis=1).astype(BF16)
+    dx[...] = dx[...] + dot_nt(dkv_ref[...], wkv[...].reshape(width, 2 * KEY_COLUMNS))
+    unit, inverse = unit_rows(u[...].astype(F32))
+    a_ref[...] = (unit * attn_gain).astype(BF16)
+    gain_ref[:, :width] = jnp.sum(dx[...] * unit, axis=0, keepdims=True)
+    grad_ref[...] = (dh[...] + unit_back(dx[...] * attn_gain, unit, inverse)).astype(BF16)
+    onward = remote(grad_ref, passed_ref, pass_send, pass_recv, place.other_section(0))
+
+    @pl.when(place.section == 1)
+    def _():
+        onward.start()
+        passed_ref[...] = jnp.zeros_like(passed_ref)
+        onward.wait_send()
+
+    @pl.when(place.section == 0)
+    def _():
+        onward.wait_recv()
+
+    scatter.drain()
+    scatter_kv.drain()
+    for copy in saves:
+        copy.wait()
+
+
+def backward_step(m, cotangent, returned, rowtab, postab, gains, weights, state_0, state_1):
+    q_all, kv_all, o_all, gu_mine, dn_mine = weights
+    rows, width = returned.shape
+    units = dn_mine.shape[0]
+    tokens = 16 * rows
+    shape = jax.ShapeDtypeStruct
+    heads = KEY_VALUE_HEADS
+    return pl.pallas_call(
+        backward_kernel,
+        out_shape=(
+            shape((rows, width), BF16),
+            shape((rows, width), BF16),
+            shape((16, rows, width), BF16),
+            shape((2 * units, tokens), BF16),
+            shape((rows, width), BF16),
+            shape((rows, width), BF16),
+            shape((rows, QUERY_COLUMNS), BF16),
+            shape((rows, 2 * KEY_COLUMNS), BF16),
+            shape(gains.shape, F32),
+        ),
+        in_specs=[SMEM] + [VMEM] * 5 + [ANY] * 5 + [ANY] * 14,
+        out_specs=[VMEM, VMEM, ANY, ANY] + [VMEM] * 5,
+        scratch_shapes=[pltpu.VMEM(w.shape, w.dtype) for w in weights]
+        + [pltpu.VMEM(w.shape, w.dtype) for w in state_0]
+        + [
+            pltpu.VMEM((16, rows, width), BF16),
+            pltpu.VMEM((2 * units, tokens), BF16),
+            pltpu.VMEM((rows, width), F32),
+            pltpu.VMEM((rows, width), F32),
+            pltpu.VMEM((heads, tokens, HEAD_SIZE), BF16),
+            pltpu.VMEM((heads, tokens, HEAD_SIZE), BF16),
+            pltpu.VMEM((QUERY_HEADS * rows, HEAD_SIZE), BF16),
+            pltpu.VMEM((QUERY_HEADS * rows, HEAD_SIZE), F32),
+            pltpu.VMEM((heads, tokens, HEAD_SIZE), F32),
+            pltpu.VMEM((heads, tokens, HEAD_SIZE), F32),
+            pltpu.VMEM((rows, tokens), F32),
+            pltpu.VMEM((16, rows, width), BF16),
+            pltpu.VMEM((8, rows, width), BF16),
+            pltpu.VMEM((8, rows, width), BF16),
+            pltpu.VMEM((16, rows, 2 * KEY_COLUMNS), BF16),
+            pltpu.VMEM((8, rows, 2 * KEY_COLUMNS), BF16),
+            pltpu.VMEM((8, rows, 2 * KEY_COLUMNS), BF16),
+            pltpu.VMEM((rows, 2 * KEY_COLUMNS), F32),
+        ]
+        + gather_sems(3)
+        + scatter_sems()
+        + scatter_sems()
+        + [
+            pltpu.SemaphoreType.DMA,
+            pltpu.SemaphoreType.DMA,
+            pltpu.SemaphoreType.DMA((7,)),
+            pltpu.SemaphoreType.DMA((7,)),
+        ],
+        compiler_params=kernel_params(2),
+    )(m, cotangent, returned, rowtab, postab, gains, *weights, *state_0, *state_1)
+
+
+def grads_kernel(*refs):
+    batches = 2
+    fwd = refs[: 2 * batches * 3]
+    bwd = refs[2 * batches * 3 : 2 * batches * 10]
+    (gq_ref, gkv_ref, go_ref, gu_out, dn_out, gains_ref,
+     e, hid, ob, df, dgu, a, da, dq, dkv, gain, pq, pkv, po, q_sib, kv_sib, o_sib, q_land, kv_land, o_land,
+     gu_stage, dn_stage, gain_all,
+     q_send, q_recv, kv_send, kv_recv, o_send, o_recv, g_send, g_recv, x_send, x_recv, local, kept) = refs[2 * batches * 10 :]
+    place = Place()
+    own = place.block()
+    ctx = place.ctx()
+    held = (ob, a, da, dq, dkv, gain, e, df, hid, dgu)
+    for section in (0, 1):
+
+        @pl.when(place.section == section)
+        def _():
+            for b in range(batches):
+                e_b, hid_b, ob_b = fwd[(section * batches + b) * 3 : (section * batches + b) * 3 + 3]
+                df_b, dgu_b, a_b, da_b, dq_b, dkv_b, gain_b = bwd[
+                    (section * batches + b) * 7 : (section * batches + b) * 7 + 7
+                ]
+                for i, src in enumerate((ob_b, a_b, da_b, dq_b, dkv_b, gain_b, e_b, df_b, hid_b, dgu_b)):
+                    load(src, held[i].at[b], kept.at[2 * i + b])
+
+    others = (1, 2, 3, 4, 5, 6, 7)
+    greet(place, others + (Z_BIT,))
+
+    def arrived(index):
+        for b in range(batches):
+            pltpu.make_async_copy(held[index].at[b], held[index].at[b], kept.at[2 * index + b]).wait()
+
+    for i in range(6):
+        arrived(i)
+    rows, width = a.shape[1:]
+    half = QUERY_COLUMNS // 2
+    lines = gain_all.shape[1]
+    total_gain = gain[0] + gain[1]
+    lanes = total_gain.shape[1] // 128
+    gain_all[own, :lanes] = jnp.concatenate([total_gain[:, i * 128 : (i + 1) * 128] for i in range(lanes)], axis=0)
+    gain_all[own, lanes:] = jnp.zeros((lines - lanes, 128), F32)
+    gain_gather = Gather(place, gain_all, row_pieces((lines,), TOWARD_Z), g_send, g_recv)
+    gain_gather.start()
+
+    def both(ref, columns):
+        return ref[:, :, columns].reshape(batches * rows, columns.size)
+
+    def outer(c, _):
+        wide = pl.ds(pl.multiple_of(c * (width // 8), width // 8), width // 8)
+        for t in range(2):
+            lead = pl.ds(t * half, half)
+            pq[t * 8 + c] = dot_tn(both(a, wide), both(dq, lead)).astype(BF16)
+            po[t * 8 + c] = dot_tn(both(ob, lead), both(da, wide)).astype(BF16)
+            narrow = pl.ds(pl.multiple_of((t * 8 + c) * (width // 16), width // 16), width // 16)
+            pkv[t * 8 + c] = dot_tn(both(a, narrow), both(dkv, pl.ds(0, 2 * KEY_COLUMNS))).astype(BF16)
+        return 0
+
+    lax.fori_loop(0, 8, outer, 0)
+
+    def putter(ref):
+        def put(index, total):
+            ref[index] = total
+
+        return put
+
+    scatters = []
+    for part, sib, land, send, recv, ref in (
+        (pq, q_sib, q_land, q_send, q_recv, gq_ref),
+        (po, o_sib, o_land, o_send, o_recv, go_ref),
+        (pkv, kv_sib, kv_land, kv_send, kv_recv, gkv_ref),
+    ):
+        tall_half = part.shape[1] // 2
+        scatters.append(
+            Scatter(place, part, sib, land, row_pieces((tall_half, tall_half), TOWARD_Z), send, recv, putter(ref))
+        )
+    for scatter in scatters:
+        scatter.start_sibling()
+    for i in range(6, 10):
+        arrived(i)
+    units = hid.shape[1]
+
+    def share(mask, back=0):
+        rows_there = pl.ds(pl.multiple_of((place.ctx(mask) if back else ctx) * units, 16), units)
+        return (gu_stage.at[mask], gu_out.at[:, rows_there, :]), (dn_stage.at[mask], dn_out.at[rows_there, :])
+
+    sent = []
+    for mask in (6, 7, 2, 3, 4, 5, 1, 0):
+        columns = pl.ds(pl.multiple_of(place.ctx(mask) * (width // 8), width // 8), width // 8)
+        gu = jnp.zeros((2 * units, width // 8), F32)
+        dn = jnp.zeros((units, width // 8), F32)
+        for b in range(batches):
+            gu = gu + dot(dgu[b], e[b, :, :, columns].reshape(16 * rows, width // 8))
+            dn = dn + dot(hid[b], df[b, :, :, columns].reshape(16 * rows, width // 8))
+        gu_stage[mask] = gu.astype(BF16).reshape(2, units, width // 8)
+        dn_stage[mask] = dn.astype(BF16)
+        for j, (src, dst) in enumerate(share(mask)):
+            slot = 2 * mask + j
+            if mask:
+                copy = remote(src, dst, x_send.at[slot], x_recv.at[slot], place.peer(mask))
+                copy.start()
+            else:
+                copy = load(src, dst, local.at[j])
+            sent.append((mask, copy))
+    for scatter in scatters:
+        scatter.add_sibling()
+        scatter.finish()
+    gain_gather.finish()
+    total = gain_all[0]
+    for i in range(1, 16):
+        total = total + gain_all[i]
+    gains_ref[...] = total
+    for mask in others:
+        for j, (src, dst) in enumerate(share(mask, 1)):
+            slot = 2 * mask + j
+            remote(src, dst, x_send.at[slot], x_recv.at[slot], place.peer(mask)).wait_recv()
+    for mask, copy in sent:
+        if mask:
+            copy.wait_send()
+        else:
+            copy.wait()
+    for scatter in scatters:
+        scatter.drain()
+
+
+def weight_grads(forward_0, forward_1, backward_0, backward_1):
+    operands = []
+    for side in (forward_0, forward_1, backward_0, backward_1):
+        for kept in side:
+            operands.extend(kept)
+    (e, hid, ob), (df, dgu, a, da, dq, dkv, gain) = forward_0[0], backward_0[0]
+    rows, width = a.shape
+    units = hid.shape[0]
+    columns = width // 8
+    lines = -(-gain.shape[1] // 1024) * 8
+    shape = jax.ShapeDtypeStruct
+    half = QUERY_COLUMNS // 2
+    parts = [(columns, half), (width // 16, 2 * KEY_COLUMNS), (half, columns)]
+    return pl.pallas_call(
+        grads_kernel,
+        out_shape=(
+            shape(parts[0], F32),
+            shape(parts[1], F32),
+            shape(parts[2], F32),
+            shape((2, 8 * units, columns), BF16),
+            shape((8 * units, columns), BF16),
+            shape((lines, 128), F32),
+        ),
+        in_specs=[ANY] * len(operands),
+        out_specs=[VMEM] * 3 + [ANY, ANY, VMEM],
+        scratch_shapes=[pltpu.VMEM((2,) + x.shape, x.dtype) for x in (e, hid, ob, df, dgu, a, da, dq, dkv, gain)]
+        + [pltpu.VMEM((16,) + x, BF16) for x in parts]
+        + [pltpu.VMEM((8,) + x, BF16) for x in parts] * 2
+        + [
+            pltpu.VMEM((8, 2, units, columns), BF16),
+            pltpu.VMEM((8, units, columns), BF16),
+            pltpu.VMEM((16, lines, 128), F32),
+        ]
+        + scatter_sems() * 3
+        + gather_sems(1)
+        + [pltpu.SemaphoreType.DMA((16,)), pltpu.SemaphoreType.DMA((16,)), pltpu.SemaphoreType.DMA((2,))]
+        + [pltpu.SemaphoreType.DMA((20,))],
+        compiler_params=kernel_params(3),
+    )(*operands)
+
+
+def cube_device(
+    inputs,
+    cotangent,
+    slot_order,
+    query_weight,
+    key_value_matrix,
+    out_weight,
+    gateup_weight,
+    down_weight,
+    norm_gains,
+):
+    section_id = lax.axis_index("section")
+    tensor_id = lax.axis_index("tensor")
+    context_id = lax.axis_index("ctx")
+    batches, rows, width = inputs.shape
+    tensors, contexts = 2, 8
+    span = rows * tensors
+    lanes = -(-norm_gains.shape[1] // 128)
+    gains_block = jnp.pad(norm_gains[0], (0, lanes * 128 - norm_gains.shape[1])).reshape(lanes, 128)
+    gains_block = jnp.pad(gains_block, ((0, -lanes % 16), (0, 0)))
+    gateup_rows = jnp.transpose(gateup_weight[0], (1, 2, 0))
+    brought = bring_weights(
+        query_weight[0], key_value_matrix[0], out_weight[0], gateup_rows, down_weight[0], gains_block
+    )
+    weights = brought[:5]
+    gains = brought[5].reshape(16, -1)[:, : norm_gains.shape[1]].reshape(1, -1).astype(F32)
+    own_slot = jnp.sum(jnp.where(jnp.arange(contexts) == context_id, slot_order, 0), axis=1)
+    own_pos = own_slot[:, None] * span + tensor_id * rows + jnp.arange(rows)[None, :]
+    half_width = HEAD_SIZE // 2
+    frequency = ROPE_BASE ** (-(jnp.arange(half_width, dtype=F32) * 2.0) / HEAD_SIZE)
+    angles = own_pos.astype(F32)[..., None] * frequency
+    cosine, sine = jnp.cos(angles), jnp.sin(angles)
+    rowtab = jnp.concatenate(
+        [cosine, cosine, -sine, sine, jnp.broadcast_to(own_pos.astype(F32)[..., None], (batches, rows, 128))], axis=-1
+    )
+    within = jnp.arange(tensors)[:, None, None] * rows + jnp.arange(rows)[None, None, :]
+    key_pos = (slot_order[:, None, :, None] * span + within[None]).reshape(batches, 1, -1)
+    postab = jnp.broadcast_to(key_pos.astype(F32), (batches, 8, key_pos.shape[-1]))
+    received = jnp.zeros_like(inputs[0])
+    kept = []
+    for step in range(batches + 1):
+        m = jnp.clip(step - section_id, 0, batches - 1).astype(jnp.int32).reshape(1)
+        out = forward_step(m, inputs, received, rowtab, postab, gains, weights)
+        kept.append(out)
+        received = out[1]
+    section_result = jnp.stack(
+        [jnp.where(section_id == 0, kept[b][0], kept[b + 1][0]) for b in range(batches)]
+    )[None]
+    returned = jnp.zeros_like(inputs[0])
+    back = []
+    for step in range(batches + 1):
+        m = jnp.clip(step - 1 + section_id, 0, batches - 1).astype(jnp.int32).reshape(1)
+        states = [kept[at][2:8] + (kept[at][10],) for at in (max(step - 1, 0), min(step + 1, batches))]
+        out = backward_step(m, cotangent, returned, rowtab, postab, gains, weights, *states)
+        back.append(out)
+        returned = out[1]
+    input_result = jnp.stack(
+        [jnp.where(section_id == 0, back[b + 1][0], back[b][0]) for b in range(batches)]
+    )[None]
+
+    def forward_kept(out):
+        return (out[9], out[11], out[8])
+
+    grad_query, grad_keyval, grad_out, grad_gateup, grad_down, grad_gains = weight_grads(
+        [forward_kept(kept[b]) for b in range(batches)],
+        [forward_kept(kept[b + 1]) for b in range(batches)],
+        [back[b + 1][2:] for b in range(batches)],
+        [back[b][2:] for b in range(batches)],
+    )
+    share = norm_gains.shape[1]
+    gains_own = lax.dynamic_slice(grad_gains.reshape(-1), ((tensor_id * contexts + context_id) * share,), (share,))
+    return (
+        section_result,
+        input_result,
+        grad_query[None],
+        grad_keyval[None],
+        grad_out[None],
+        jnp.transpose(grad_gateup, (2, 0, 1)).astype(F32)[None],
+        grad_down.astype(F32)[None],
+        gains_own[None],
+    )
+
+
+def fits_cube(mesh):
+    return mesh.shape["section"] == 2 and mesh.shape["tensor"] == 2 and mesh.shape["ctx"] == 8
+
+
 def solution(mesh):
     return jax.shard_map(
-        per_device,
+        cube_device if fits_cube(mesh) else per_device,
         mesh=mesh,
         in_specs=(
             P(None, ("tensor", "ctx"), None),

time: 1690 us -> 853 us (0.50)
  waiting for transfers between devices: 846 us -> 0 us
  Pallas kernels: 0 us -> 810 us
  matrix products: 253 us -> 0 us
  blocking collectives: 223 us -> 0 us
  local copies, waits for them, and re-layouts: 203 us -> 24.8 us
  other arithmetic: 120 us -> 8.18 us
  between operations: 21.9 us -> 1.33 us
    pallas_call x0 -> x8, Pallas kernels: none -> 810 us  [the longest x3 283 us: backward_step(): pl.pallas_call(backward_kernel, out_shape=(shape((rows, width), BF16), sh...]
    reduce_scatter x16 -> x0, waiting for transfers between devices: 309 us -> none  [the longest x12 113 us: scatter_rows(): lax.psum_scatter(values.astype(jnp.bfloat16), 'tensor', scatter_dimension...]
    unnamed x32 -> x0, waiting for transfers between devices: 308 us -> none
    dot_general x119 -> x0, matrix products: 253 us -> none  [the longest x5 36.4 us: row_product(): lax.dot_general(left_rows, right_rows, (((0,), (0,)), ((), ())), preferre...]
    all_gather x8 -> x0, waiting for transfers between devices: 189 us -> none  [the longest x1 96.9 us: per_device(): gateup_full = lax.all_gather(gateup_weight[0], 'ctx', axis=0, tiled=True)]
    all_gather x12 -> x0, blocking collectives: 114 us -> none  [gather_rows(): return lax.all_gather(values, 'tensor', axis=0, tiled=True)]
    unnamed x2 -> x0, blocking collectives: 109 us -> none
    unnamed x488 -> x28, local copies, waits for them, and re-layouts: 69.7 us -> 19.6 us
  transfers between devices with their start and end apart: 32 -> 0, of which waited for: 27 -> 0; matrix products, arithmetic and copies ran while one was open for 16% -> 0% of each run, Pallas kernels for 0% -> 0%
where the time goes in v1:
time: 853 us; the launch traced here: 844 us
  Pallas kernels  810 us (95%)
  local copies, waits for them, and re-layouts  24.8 us (3%)
    pallas_call x3, Pallas kernels, backward_step(): pl.pallas_call(backward_kernel, out_shape=(shape((rows, width), BF16), sh...  283 us
    pallas_call x3, Pallas kernels, forward_step(): pl.pallas_call(forward_kernel, out_shape=(shape((rows, width), BF16), sha...  242 us
    pallas_call x1, Pallas kernels, bring_weights(): pl.pallas_call(weights_kernel, out_shape=(shape((16,) + query.shape, BF16...  155 us
    pallas_call x1, Pallas kernels, weight_grads(): pl.pallas_call(grads_kernel, out_shape=(shape(parts[0], F32), shape(parts...  131 us
    unnamed x28, local copies, waits for them, and re-layouts  19.6 us

profile of v1, /device:TPU:0, one launch (start us, length us, event | category | flops | bytes accessed | tf_op | source)
XLA Modules:
  0.0 844.2 jit_solution(11480524870123428081)
XLA Ops:
  0.7 0.1 iota_add_fusion
  0.8 0.7 reduce
  1.5 0.8 broadcast_multiply_fusion
  2.3 0.1 add_convert_fusion.1
  2.4 0.6 pad.9.g_ref
  3.0 0.1 add.95
  3.0 0.1 add.89
  3.1 0.1 add.90
  3.2 0.6 broadcast_in_dim.60.postab
  3.8 0.1 broadcast_in_dim.59
  3.9 0.3 multiply_sine_fusion
  4.2 0.8 concatenate.3.rowtab
  5.0 7.3 copy.17
  12.3 154.6 %shard_map.152 = (bf16[16,256,640]{2,1,0:T(8,128)(2,1)}, bf16[16,128,640]{2,1,0:T(8,128)(2,1)}, bf16[16,640,256]{2,1,0:T(8,128)(2,1)}, bf16[2,320,2048]{2,1,0:T(...) custom-call(bf16[256,640]{1,0:T(8,128)(2,1)} %bitcast.49, bf16[128,640]{1,0:T(8,128)(2,1)} %bitcast.51, ...), custom_call_target="tpu_custom_call" | custom-call | tf_op jit(solution)/shard_map/pallas_call | solution.py:806
  167.0 0.9 copy.21
  167.9 0.7 reshape.156.gains
  168.6 0.7 broadcast_4_received_ref_returned_ref.2.received_ref.returned_ref
  169.3 79.3 %shard_map.153 = (bf16[64,2048]{1,0:T(8,128)(2,1)}, bf16[64,2048]{1,0:T(8,128)(2,1)}, bf16[64,2048]{1,0:T(8,128)(2,1)}, f32[64,2048]{1,0:T(8,128)}, f32[1280,64]...) custom-call(s32[1]{0:T(128)} %bitcast.m_ref, ...), custom_call_target="tpu_custom_call" | custom-call | tf_op jit(solution)/shard_map/pallas_call | solution.py:1022
  248.6 84.8 %shard_map.154 = (bf16[64,2048]{1,0:T(8,128)(2,1)}, bf16[64,2048]{1,0:T(8,128)(2,1)}, bf16[64,2048]{1,0:T(8,128)(2,1)}, f32[64,2048]{1,0:T(8,128)}, f32[1280,64]...) custom-call(s32[1]{0:T(128)} %bitcast.8.m_ref, ...), custom_call_target="tpu_custom_call" | custom-call | tf_op jit(solution)/shard_map/pallas_call | solution.py:1022
  333.4 97.1 %shard_map.156 = (bf16[64,2048]{1,0:T(8,128)(2,1)}, bf16[64,2048]{1,0:T(8,128)(2,1)}, bf16[16,64,2048]{2,1,0:T(8,128)(2,1)}, bf16[640,1024]{1,0:T(8,128)(2,1)}, ...) custom-call(s32[1]{0:T(128)} %bitcast.14.m_ref, ...), custom_call_target="tpu_custom_call" | custom-call | tf_op jit(solution)/shard_map/pallas_call | solution.py:1224
  430.6 77.4 %shard_map.155 = (bf16[64,2048]{1,0:T(8,128)(2,1)}, bf16[64,2048]{1,0:T(8,128)(2,1)}, bf16[64,2048]{1,0:T(8,128)(2,1)}, f32[64,2048]{1,0:T(8,128)}, f32[1280,64]...) custom-call(s32[1]{0:T(128)} %bitcast.10.m_ref, ...), custom_call_target="tpu_custom_call" | custom-call | tf_op jit(solution)/shard_map/pallas_call | solution.py:1022
  508.0 97.0 %shard_map.157 = (bf16[64,2048]{1,0:T(8,128)(2,1)}, bf16[64,2048]{1,0:T(8,128)(2,1)}, bf16[16,64,2048]{2,1,0:T(8,128)(2,1)}, bf16[640,1024]{1,0:T(8,128)(2,1)}, ...) custom-call(s32[1]{0:T(128)} %bitcast.13.m_ref, ...), custom_call_target="tpu_custom_call" | custom-call | tf_op jit(solution)/shard_map/pallas_call | solution.py:1224
  605.0 88.9 %shard_map.158 = (bf16[64,2048]{1,0:T(8,128)(2,1)}, bf16[64,2048]{1,0:T(8,128)(2,1)}, bf16[16,64,2048]{2,1,0:T(8,128)(2,1)}, bf16[640,1024]{1,0:T(8,128)(2,1)}, ...) custom-call(s32[1]{0:T(128)} %bitcast.16.m_ref, ...), custom_call_target="tpu_custom_call" | custom-call | tf_op jit(solution)/shard_map/pallas_call | solution.py:1224
  693.9 0.0 copy-start.5
  693.9 0.0 copy-start.6
  693.9 0.0 copy-start.7
  693.9 0.0 copy-start.8
  693.9 0.0 copy-start.9
  693.9 0.0 copy-start.10
  693.9 130.7 %shard_map.159 = (f32[256,640]{1,0:T(8,128)}, f32[128,640]{1,0:T(8,128)}, f32[640,256]{1,0:T(8,128)}, bf16[2,2560,256]{2,1,0:T(8,128)(2,1)}, bf16[2560,256]{1,0:T(8,128)(2,1)}, /*index=5*/f32[40,128]{1,0:T(8,128)}) custom-call(bf16[16,64,2048]{2,1,0:T(8,128)(2,1)} %get-tuple-element.118.refs_0_, bf16[320,1024]{1,0:T(8,128)(2,1)} %get-tuple-element.119.refs_1_, ...), custom_call_target="tpu_custom_call" | custom-call | tf_op jit(solution)/shard_map/pallas_call | solution.py:1410
  824.6 0.0 copy-start.1
  824.6 0.0 copy-done.5
  824.7 0.0 copy-done.6
  824.7 0.0 copy-done.7
  824.7 0.0 copy-done.8
  824.7 0.0 copy-done.9
  824.7 0.0 copy-done.10
  824.7 0.1 select_bitcast_fusion.1
  824.8 0.8 maximum_bitcast_fusion.1
  825.6 0.0 copy-start
  825.7 0.9 dynamic_slice.3
  826.6 0.6 broadcast_in_dim.70
  827.1 0.8 maximum_bitcast_fusion
  828.0 0.0 copy-done.1
  828.0 1.7 bitcast_convert_fusion
  829.7 0.0 copy-done
  829.7 2.7 convert_bitcast_fusion
  832.4 0.0 copy-start.3
  832.4 0.0 copy-start.4
  832.4 0.0 copy-start.2
  832.4 8.9 %copy.18 = f32[1,256,2,2560]{3,2,1,0:T(2,128)} copy(f32[1,256,2,2560]{1,3,2,0:T(8,128)} %convert_bitcast_fusion) | data formatting | bytes 10485760
  841.3 0.0 copy-done.3
  841.3 0.8 copy.25
  842.2 0.0 copy-done.4
  842.2 0.7 copy.26
  842.9 0.0 copy-done.2
  842.9 0.8 copy.27
  (8 shorter events, 0.1 us)
Async XLA Ops:
  693.9 130.8 %copy-start.5 = (bf16[64,2048]{1,0:T(8,128)(2,1)S(1)}, bf16[64,2048]{1,0:T(8,128)(2,1)}, u32[]{:S(2)}) copy-start(bf16[64,2048]{1,0:T(8,128)(2,1)} %get-tuple-element.87) | copy-start | bytes 786436
  693.9 130.8 %copy-start.6 = (bf16[64,2048]{1,0:T(8,128)(2,1)S(1)}, bf16[64,2048]{1,0:T(8,128)(2,1)}, u32[]{:S(2)}) copy-start(bf16[64,2048]{1,0:T(8,128)(2,1)} %get-tuple-element.89) | copy-start | bytes 786436
  693.9 130.8 %copy-start.7 = (bf16[64,2048]{1,0:T(8,128)(2,1)S(1)}, bf16[64,2048]{1,0:T(8,128)(2,1)}, u32[]{:S(2)}) copy-start(bf16[64,2048]{1,0:T(8,128)(2,1)} %get-tuple-element.115) | copy-start | bytes 786436
  693.9 130.8 %copy-start.8 = (bf16[64,2048]{1,0:T(8,128)(2,1)S(1)}, bf16[64,2048]{1,0:T(8,128)(2,1)}, u32[]{:S(2)}) copy-start(bf16[64,2048]{1,0:T(8,128)(2,1)} %get-tuple-element.91) | copy-start | bytes 786436
  693.9 130.8 %copy-start.9 = (bf16[64,2048]{1,0:T(8,128)(2,1)S(1)}, bf16[64,2048]{1,0:T(8,128)(2,1)}, u32[]{:S(2)}) copy-start(bf16[64,2048]{1,0:T(8,128)(2,1)} %get-tuple-element.114) | copy-start | bytes 786436
  693.9 130.8 %copy-start.10 = (bf16[64,2048]{1,0:T(8,128)(2,1)S(1)}, bf16[64,2048]{1,0:T(8,128)(2,1)}, u32[]{:S(2)}) copy-start(bf16[64,2048]{1,0:T(8,128)(2,1)} %get-tuple-element.117) | copy-start | bytes 786436
  824.6 3.3 copy-start.1
  825.6 4.0 copy-start
  832.4 8.9 %copy-start.3 = (f32[256,640]{1,0:T(8,128)S(1)}, f32[256,640]{1,0:T(8,128)}, u32[]{:S(2)}) copy-start(f32[256,640]{1,0:T(8,128)} %get-tuple-element.148) | copy-start | bytes 1966084
  832.4 9.8 %copy-start.4 = (f32[128,640]{1,0:T(8,128)S(1)}, f32[128,640]{1,0:T(8,128)}, u32[]{:S(2)}) copy-start(f32[128,640]{1,0:T(8,128)} %get-tuple-element.149) | copy-start | bytes 983044
  832.4 10.5 %copy-start.2 = (f32[640,256]{1,0:T(8,128)S(1)}, f32[640,256]{1,0:T(8,128)}, u32[]{:S(2)}) copy-start(f32[640,256]{1,0:T(8,128)} %get-tuple-element.150) | copy-start | bytes 1966084

commit v2 on v0

--- a/solution.py
+++ b/solution.py
@@ -1,6 +1,10 @@
+import typing
+
 import jax
 import jax.numpy as jnp
 from jax import lax
+from jax.experimental import pallas as pl
+from jax.experimental.pallas import tpu as pltpu
 from jax.sharding import PartitionSpec as P
 
 MODEL_WIDTH = 2048
@@ -505,9 +509,1608 @@
     )
 
 
+C_BIT, X_BIT, Y_BIT, Z_BIT = 1, 2, 4, 8
+MESH_ID = pl.DeviceIdType.MESH
+F32 = jnp.float32
+BF16 = jnp.bfloat16
+GROUP = QUERY_HEADS // KEY_VALUE_HEADS
+KEY_COLUMNS = KEY_VALUE_HEADS * HEAD_SIZE
+QUERY_COLUMNS = QUERY_HEADS * HEAD_SIZE
+HALF_COLUMNS = QUERY_COLUMNS // 2
+SCALE = HEAD_SIZE ** (-0.5)
+VMEM_BYTES = 62 * 2**20
+CYCLES = ((X_BIT, Y_BIT, Z_BIT), (Y_BIT, Z_BIT, X_BIT), (Z_BIT, X_BIT, Y_BIT))
+TOWARD_Z = ((X_BIT, Y_BIT, Z_BIT), (Y_BIT, X_BIT, Z_BIT))
+ROW_WIDTHS = (768, 640, 640)
+KV_WIDTHS = (256, 256, 128)
+class Place:
+    def __init__(self):
+        self.section = lax.axis_index("section")
+        ctx = lax.axis_index("ctx")
+        self.bits = (ctx % 2, (ctx // 2) % 2, ctx // 4, lax.axis_index("tensor"))
+
+    def flipped(self, mask):
+        return [1 - bit if mask & (1 << i) else bit for i, bit in enumerate(self.bits)]
+
+    def block(self, mask=0):
+        core, x, y, z = self.flipped(mask)
+        return z * 8 + y * 4 + x * 2 + core
+
+    def chip(self, mask=0):
+        _, x, y, z = self.flipped(mask)
+        return z * 4 + y * 2 + x
+
+    def ctx(self, mask=0):
+        core, x, y, _ = self.flipped(mask)
+        return y * 4 + x * 2 + core
+
+    def peer(self, mask):
+        core, x, y, z = self.flipped(mask)
+        return (self.section, z, y * 4 + x * 2 + core)
+
+    def other_section(self, section):
+        core, x, y, z = self.bits
+        return (section, z, y * 4 + x * 2 + core)
+
+
+def remote(src, dst, send, recv, device):
+    return pltpu.make_async_remote_copy(
+        src_ref=src, dst_ref=dst, send_sem=send, recv_sem=recv, device_id=device, device_id_type=MESH_ID
+    )
+
+
+def load(src, dst, sem):
+    copy = pltpu.make_async_copy(src, dst, sem)
+    copy.start()
+    return copy
+
+
+def landed(ref, sem):
+    pltpu.make_async_copy(ref, ref, sem).wait()
+
+
+def greet(place, masks, into=None):
+    barrier = pltpu.get_barrier_semaphore()
+    for mask in masks:
+        pl.semaphore_signal(barrier, inc=1, device_id=place.peer(mask), device_id_type=MESH_ID)
+    if into is None:
+        pl.semaphore_wait(barrier, len(masks))
+        return
+    if into == "both":
+        pl.semaphore_signal(
+            barrier, inc=1, device_id=place.other_section(1 - place.section), device_id_type=MESH_ID
+        )
+        pl.semaphore_wait(barrier, len(masks) + 1)
+        return
+
+    @pl.when(place.section == into)
+    def _():
+        pl.semaphore_signal(barrier, inc=1, device_id=place.other_section(1 - into), device_id_type=MESH_ID)
+        pl.semaphore_wait(barrier, len(masks))
+
+    @pl.when(place.section != into)
+    def _():
+        pl.semaphore_wait(barrier, len(masks) + 1)
+
+
+def column_pieces(widths, orders):
+    start, pieces = 0, []
+    for width, order in zip(widths, orders):
+        pieces.append(((slice(None), pl.ds(start, width)), order))
+        start += width
+    return pieces
+
+
+def row_pieces(heights, orders):
+    start, pieces = 0, []
+    for height, order in zip(heights, orders):
+        pieces.append(((pl.ds(start, height), slice(None)), order))
+        start += height
+    return pieces
+
+
+def halves(rows):
+    return row_pieces((rows // 2, rows // 2), TOWARD_Z)
+
+
+class Gather:
+    def __init__(self, place, buf, pieces, sems, siblings):
+        self.place, self.buf, self.pieces, self.siblings = place, buf, list(enumerate(pieces)), siblings
+        self.send, self.recv = sems
+
+    def _where(self, piece, mask):
+        block = self.place.block(mask) if self.siblings else self.place.chip(mask)
+        return self.buf.at[(block,) + self.pieces[piece][1][0]]
+
+    def _copy(self, piece, mask, dim):
+        where = self._where(piece, mask)
+        return remote(where, where, self.send, self.recv.at[self._slot(piece, mask ^ dim)], self.place.peer(dim))
+
+    def _slot(self, piece, mask):
+        return piece * 15 + mask - 1 if self.siblings else piece * 7 + mask // 2 - 1
+
+    def _start(self, piece, mask, dim):
+        self._copy(piece, mask, dim).start()
+
+    def _arrived(self, piece, mask, dim):
+        where = self._where(piece, mask)
+        remote(where, where, self.send, self.recv.at[self._slot(piece, mask)], self.place.peer(dim)).wait_recv()
+
+    def _pass(self, piece, mask, dims):
+        for dim in dims:
+            self._start(piece, mask, dim)
+        if self.siblings:
+            self._start(piece, mask, C_BIT)
+
+    def start(self):
+        for turn in range(3):
+            for piece, (_, order) in self.pieces:
+                self._start(piece, 0, order[turn])
+        if self.siblings:
+            for piece, _ in self.pieces:
+                self._start(piece, 0, C_BIT)
+
+    def first(self):
+        for piece, (_, (d0, d1, d2)) in self.pieces:
+            self._arrived(piece, d0, d0)
+            self._pass(piece, d0, (d1, d2))
+
+    def second(self):
+        for part in (0, 1):
+            for piece, (_, (d0, d1, d2)) in self.pieces:
+                mask = (d1, d0 ^ d1)[part]
+                self._arrived(piece, mask, d1)
+                self._pass(piece, mask, (d2,))
+
+    def third(self):
+        for part in (0, 1, 2, 3):
+            for piece, (_, (d0, d1, d2)) in self.pieces:
+                mask = (d2, d0 ^ d2, d1 ^ d2, d0 ^ d1 ^ d2)[part]
+                self._arrived(piece, mask, d2)
+                self._pass(piece, mask, ())
+
+    def last(self):
+        if self.siblings:
+            for piece, _ in self.pieces:
+                for mask in range(0, 16, 2):
+                    self._arrived(piece, mask ^ C_BIT, C_BIT)
+
+    def finish(self):
+        self.first()
+        self.second()
+        self.third()
+        self.last()
+
+    def drain(self):
+        landed(self.buf.at[pl.ds(0, 15 if self.siblings else 7)], self.send)
+
+
+class Scatter:
+    def __init__(self, place, part, land, pieces, sems, put, sib_land=None):
+        self.place, self.part, self.land, self.sib_land = place, part, land, sib_land
+        self.pieces, self.put = list(enumerate(pieces)), put
+        self.send, self.recv = sems
+
+    def _block(self, mask):
+        return self.place.chip(mask) if self.sib_land is None else self.place.block(mask)
+
+    def _sib(self, i, mask):
+        return remote(
+            self.part.at[self.place.block(mask | C_BIT)],
+            self.sib_land.at[i],
+            self.send,
+            self.recv.at[len(self.pieces) * 7 + i],
+            self.place.peer(C_BIT),
+        )
+
+    def siblings(self):
+        masks = (14, 12, 10, 6, 8, 4, 2, 0)
+        for i, mask in enumerate(masks):
+            self._sib(i, mask).start()
+        for i, mask in enumerate(masks):
+            self._sib(i, mask).wait_recv()
+            block = self.place.block(mask)
+            self.part[block] = (self.part[block].astype(F32) + self.sib_land[i].astype(F32)).astype(BF16)
+
+    def _copy(self, piece, mask, dim):
+        index = self.pieces[piece][1][0]
+        return remote(
+            self.part.at[(self._block(mask),) + index],
+            self.land.at[(mask // 2 - 1,) + index],
+            self.send,
+            self.recv.at[piece * 7 + mask // 2 - 1],
+            self.place.peer(dim),
+        )
+
+    def _start(self, piece, mask, dim):
+        self._copy(piece, mask, dim).start()
+
+    def _sum(self, piece, mask, dim):
+        self._copy(piece, mask, dim).wait_recv()
+        index = self.pieces[piece][1][0]
+        at = (self._block(mask ^ dim),) + index
+        return at, self.part[at].astype(F32) + self.land[(mask // 2 - 1,) + index].astype(F32)
+
+    def _add(self, piece, mask, dim):
+        at, total = self._sum(piece, mask, dim)
+        self.part[at] = total.astype(BF16)
+
+    def start(self, ready=range(16), pieces=None):
+        for part in (0, 1, 2, 3):
+            for piece, (_, (d0, d1, d2)) in self.pieces if pieces is None else [self.pieces[i] for i in pieces]:
+                mask = (d0 ^ d1 ^ d2, d1 ^ d2, d0 ^ d2, d2)[part]
+                if mask in ready:
+                    self._start(piece, mask, d2)
+
+    def second(self):
+        for part in (0, 1):
+            for piece, (_, (d0, d1, d2)) in self.pieces:
+                mask = (d0 ^ d1, d1)[part]
+                self._add(piece, mask ^ d2, d2)
+                self._start(piece, mask, d1)
+        for piece, (_, (d0, d1, d2)) in self.pieces:
+            self._add(piece, d0 ^ d2, d2)
+
+    def third(self):
+        for piece, (_, (d0, d1, d2)) in self.pieces:
+            self._add(piece, d0 ^ d1, d1)
+            self._start(piece, d0, d0)
+        for piece, (_, (d0, d1, d2)) in self.pieces:
+            self._add(piece, d2, d2)
+        for piece, (_, (d0, d1, d2)) in self.pieces:
+            self._add(piece, d1, d1)
+
+    def last(self):
+        for piece, (index, (d0, d1, d2)) in self.pieces:
+            _, total = self._sum(piece, d0, d0)
+            self.put(index, total)
+
+    def finish(self):
+        self.second()
+        self.third()
+        self.last()
+
+    def drain(self):
+        landed(self.part.at[pl.ds(0, 7 if self.sib_land is None else 15)], self.send)
+
+
+def sems(count):
+    return [pltpu.SemaphoreType.DMA((count,)), pltpu.SemaphoreType.DMA((count,))]
+
+
+def pair(count):
+    return [pltpu.SemaphoreType.DMA, pltpu.SemaphoreType.DMA((count,))]
+
+
+class Refs(dict):
+    __getattr__ = dict.__getitem__
+
+
+class Out(typing.NamedTuple):
+    shape: tuple
+    dtype: typing.Any
+    far: bool
+
+
+class In(typing.NamedTuple):
+    array: typing.Any
+    far: bool
+
+
+def named(tree):
+    if isinstance(tree, dict):
+        return Refs({name: named(value) for name, value in tree.items()})
+    return [named(value) for value in tree] if isinstance(tree, list) else tree
+
+
+def near(**arrays):
+    return {name: In(array, False) for name, array in arrays.items()}
+
+
+def far(**arrays):
+    return {name: In(array, True) for name, array in arrays.items()}
+
+
+def run(body, collective, inputs, outputs, scratch):
+    def is_leaf(value):
+        return not isinstance(value, (dict, list))
+
+    trees = [jax.tree.flatten(tree, is_leaf=is_leaf) for tree in (inputs, outputs, scratch)]
+    (given, made, held) = [leaves for leaves, _ in trees]
+
+    def kernel(*refs):
+        parts, start = [], 0
+        for leaves, tree in trees:
+            parts.append(named(jax.tree.unflatten(tree, refs[start : start + len(leaves)])))
+            start += len(leaves)
+        body(*parts)
+
+    def specs(leaves):
+        return [pl.BlockSpec(memory_space=pl.ANY if leaf.far else pltpu.VMEM) for leaf in leaves]
+
+    results = pl.pallas_call(
+        kernel,
+        out_shape=tuple(jax.ShapeDtypeStruct(leaf.shape, leaf.dtype) for leaf in made),
+        in_specs=specs(given),
+        out_specs=tuple(specs(made)),
+        scratch_shapes=held,
+        compiler_params=pltpu.CompilerParams(
+            collective_id=collective, has_side_effects=True, vmem_limit_bytes=VMEM_BYTES
+        ),
+    )(*[leaf.array for leaf in given])
+    return jax.tree.unflatten(trees[1][1], results)
+
+
+def dot(left, right):
+    return lax.dot_general(left, right, (((1,), (0,)), ((), ())), preferred_element_type=F32)
+
+
+def dot_nt(left, right):
+    return lax.dot_general(left, right, (((1,), (1,)), ((), ())), preferred_element_type=F32)
+
+
+def dot_tn(left, right):
+    return lax.dot_general(left, right, (((0,), (0,)), ((), ())), preferred_element_type=F32)
+
+
+def unit_rows(values):
+    inverse = lax.rsqrt(jnp.mean(values * values, axis=-1, keepdims=True) + EPSILON)
+    return values * inverse, inverse
+
+
+def unit_back(scaled, unit, inverse):
+    return inverse * (scaled - unit * jnp.mean(scaled * unit, axis=-1, keepdims=True))
+
+
+def stack_heads(values, heads):
+    return jnp.concatenate([values[:, h * HEAD_SIZE : (h + 1) * HEAD_SIZE] for h in range(heads)], axis=0)
+
+
+def spread_heads(values, heads):
+    rows = values.shape[0] // heads
+    return jnp.concatenate([values[h * rows : (h + 1) * rows] for h in range(heads)], axis=1)
+
+
+def turned(values):
+    half = HEAD_SIZE // 2
+    return jnp.concatenate([values[:, half:], values[:, :half]], axis=1)
+
+
+def tall(rows, times):
+    return jnp.concatenate([rows] * times, axis=0)
+
+
+def rope(values, cos, sin, heads):
+    return values * tall(cos, heads) + turned(values) * tall(sin, heads)
+
+
+def unrope(values, cos, sin, heads):
+    return values * tall(cos, heads) - turned(values) * tall(sin, heads)
+
+
+def mask_bias(m, r, bias):
+    bias[...] = jnp.where(r.postab[m, 0:1, :] <= r.rowtab[m, :, 2 * HEAD_SIZE : 2 * HEAD_SIZE + 1], 0.0, -jnp.inf)
+
+
+def split_keys(kv, k5, v5):
+    rows = kv.shape[0] * kv.shape[1]
+    for g in range(KEY_VALUE_HEADS):
+        k5[g] = kv[:, :, g * HEAD_SIZE : (g + 1) * HEAD_SIZE].reshape(rows, HEAD_SIZE)
+        v5[g] = kv[:, :, KEY_COLUMNS + g * HEAD_SIZE : KEY_COLUMNS + (g + 1) * HEAD_SIZE].reshape(rows, HEAD_SIZE)
+
+
+def probabilities(queries, keys, bias):
+    scores = dot_nt(queries, keys) + tall(bias, GROUP)
+    raised = jnp.exp(scores - jnp.max(scores, axis=-1, keepdims=True))
+    return raised / jnp.sum(raised, axis=-1, keepdims=True)
+
+
+def gain_parts(r, width):
+    return (
+        r.gains[:, :width],
+        r.gains[:, width : 2 * width],
+        r.gains[:, 2 * width : 2 * width + HEAD_SIZE],
+        r.gains[:, 2 * width + HEAD_SIZE :],
+    )
+
+
+class Courier:
+    def __init__(self, place, source, target, pair, into):
+        self.place, self.into = place, into
+        self.copy = remote(source, target, pair[0], pair[1], place.other_section(into))
+
+    def start(self):
+        @pl.when(self.place.section != self.into)
+        def _():
+            self.copy.start()
+
+    def arrive(self):
+        @pl.when(self.place.section == self.into)
+        def _():
+            self.copy.wait_recv()
+
+    def leave(self):
+        @pl.when(self.place.section != self.into)
+        def _():
+            self.copy.wait_send()
+
+
+BLOCKS = 8
+KEY_PADDED = -(-KEY_COLUMNS // 128) * 128
+
+
+def unit_blocks(units):
+    return [pl.ds(half * (units // 2), units // 2) for half in (0, 1)]
+
+
+def column_blocks(width):
+    return [pl.ds(part * (width // 4), width // 4) for part in range(4)]
+
+
+def forward_kept(rows, width, units):
+    tokens = BLOCKS * rows
+    return dict(
+        u=Out((rows, width), BF16, True),
+        h=Out((rows, width), F32, True),
+        qraw=Out((rows, QUERY_COLUMNS), F32, True),
+        kraw=Out((rows, KEY_PADDED), F32, True),
+        q=Out((rows, QUERY_COLUMNS), BF16, True),
+        kv=Out((2 * BLOCKS, rows, 2 * KEY_COLUMNS), BF16, True),
+        gu=Out((2 * units, tokens), F32, True),
+        ob=Out((rows, QUERY_COLUMNS), BF16, True),
+        e=Out((BLOCKS, rows, width), BF16, True),
+        hid=Out((units, tokens), BF16, True),
+    )
+
+
+def held_like(outs):
+    return {name: pltpu.VMEM(out.shape, out.dtype) for name, out in outs.items()}
+
+
+def forward_scratch(rows, width, units):
+    return held_like(forward_kept(rows, width, units)) | dict(
+        q5=pltpu.VMEM((KEY_VALUE_HEADS, GROUP * rows, HEAD_SIZE), BF16),
+        part=pltpu.VMEM((BLOCKS, rows, width), BF16),
+        land=pltpu.VMEM((BLOCKS - 1, rows, width), BF16),
+        kv_sems=pair(45),
+        e_sems=pair(21),
+        y_sems=pair(21),
+        keep=pltpu.SemaphoreType.DMA((10,)),
+    )
+
+
+def forward_steps(r, place, m, need):
+    rows, width = r.u.shape
+    units = r.hid.shape[0]
+    attn_gain, ffn_gain, q_gain, k_gain = gain_parts(r, width)
+    cos, sin = r.rowtab[m, :, :HEAD_SIZE], r.rowtab[m, :, HEAD_SIZE : 2 * HEAD_SIZE]
+    saves = []
+
+    def keep(name):
+        saves.append(load(r[name], r.kept[name], r.keep.at[len(saves)]))
+
+    r.u[...] = r.inputs[m] if r.received is None else jnp.where(place.section == 0, r.inputs[m], r.received[...])
+    keep("u")
+    a = (unit_rows(r.u[...].astype(F32))[0] * attn_gain).astype(BF16)
+    need("keyval")
+    kv_raw = dot(a, r.w.keyval[...].reshape(width, 2 * KEY_COLUMNS))
+    r.kraw[...] = kv_raw[:, :KEY_PADDED]
+    k_raw = stack_heads(kv_raw[:, :KEY_COLUMNS], KEY_VALUE_HEADS)
+    k_low = rope(unit_rows(k_raw)[0] * k_gain, cos, sin, KEY_VALUE_HEADS).astype(BF16)
+    r.kv[place.block()] = jnp.concatenate(
+        [spread_heads(k_low, KEY_VALUE_HEADS), kv_raw[:, KEY_COLUMNS:].astype(BF16)], axis=1
+    )
+    kv_gather = Gather(place, r.kv, column_pieces(KV_WIDTHS, CYCLES), r.kv_sems, True)
+    kv_gather.start()
+    keep("kraw")
+    need("query")
+    q_raw = jnp.concatenate([dot(a, r.w.query[8 * t : 8 * t + 8].reshape(width, HALF_COLUMNS)) for t in range(2)], axis=1)
+    r.qraw[...] = q_raw
+    keep("qraw")
+    q_unit = unit_rows(stack_heads(q_raw, QUERY_HEADS))[0]
+    q_low = (rope(q_unit * q_gain, cos, sin, QUERY_HEADS) * SCALE).astype(BF16)
+    r.q5[...] = q_low.reshape(KEY_VALUE_HEADS, GROUP * rows, HEAD_SIZE)
+    r.q[...] = spread_heads(q_low, QUERY_HEADS)
+    keep("q")
+    yield
+    kv_gather.first()
+    yield
+    kv_gather.second()
+    yield
+    kv_gather.third()
+    kv_gather.last()
+    keep("kv")
+
+    def attention(k5, v5, o5, bias):
+        mask_bias(m, r, bias)
+        split_keys(r.kv, k5, v5)
+
+        def attend(g, _):
+            low = probabilities(r.q5[g], k5[g], bias[...]).astype(BF16)
+            o5[g] = dot(low, v5[g])
+            return 0
+
+        lax.fori_loop(0, KEY_VALUE_HEADS, attend, 0)
+        r.ob[...] = spread_heads(o5[...].reshape(QUERY_HEADS * rows, HEAD_SIZE), QUERY_HEADS).astype(BF16)
+
+    keys = 2 * BLOCKS * rows
+    group = pltpu.VMEM((KEY_VALUE_HEADS, keys, HEAD_SIZE), BF16)
+    mixed_heads = pltpu.VMEM((KEY_VALUE_HEADS, GROUP * rows, HEAD_SIZE), F32)
+    pl.run_scoped(attention, group, group, mixed_heads, pltpu.VMEM((rows, keys), F32))
+    keep("ob")
+    need("out")
+    for c in range(8):
+        block = pl.ds(c * (width // 8), width // 8)
+        mixed = dot(r.ob[:, :HALF_COLUMNS], r.w.out[c]) + dot(r.ob[:, HALF_COLUMNS:], r.w.out[8 + c])
+        r.h[:, block] = r.u[:, block].astype(F32) + mixed
+    keep("h")
+    r.e[place.chip()] = (unit_rows(r.h[...])[0] * ffn_gain).astype(BF16)
+    e_gather = Gather(place, r.e, column_pieces(ROW_WIDTHS, CYCLES), r.e_sems, False)
+    e_gather.start()
+    need("ffn")
+    yield
+    e_gather.first()
+    yield
+    e_gather.second()
+    yield
+    e_gather.third()
+    keep("e")
+
+    def put(index, total):
+        r.result[index] = (r.h[index] + total).astype(BF16)
+
+    scatter = Scatter(place, r.part, r.land, column_pieces(ROW_WIDTHS, CYCLES), r.y_sems, put)
+    for flip in (Z_BIT, 0):
+        first = place.chip(flip) // 4 * 4
+        tokens = pl.ds(pl.multiple_of(first * rows, 4 * rows), 4 * rows)
+        here = pl.ds(first, 4)
+        for some in unit_blocks(units):
+            gate = dot_nt(r.w.ffn[0, some], r.e[here].reshape(4 * rows, width))
+            up = dot_nt(r.w.ffn[1, some], r.e[here].reshape(4 * rows, width))
+            r.gu[some, tokens] = gate
+            r.gu[pl.ds(units + some.start, some.size), tokens] = up
+            r.hid[some, tokens] = (gate * jax.nn.sigmoid(gate) * up).astype(BF16)
+        for some in column_blocks(width):
+            outward = dot_tn(r.hid[:, tokens], r.w.ffn[2, :, some])
+            r.part[here, :, some] = outward.astype(BF16).reshape(4, rows, some.size)
+        yield
+        scatter.start([flip ^ mask for mask in (0, X_BIT, Y_BIT, X_BIT | Y_BIT)])
+        yield
+    keep("gu")
+    keep("hid")
+    scatter.second()
+    yield
+    scatter.third()
+    yield
+    scatter.last()
+    yield "result"
+    for gather in (kv_gather, e_gather):
+        gather.drain()
+    scatter.drain()
+    for copy in saves:
+        copy.wait()
+
+
+def take(steps, count):
+    for _ in range(count):
+        next(steps, None)
+
+
+def until(steps, what):
+    for said in steps:
+        if what is not None and said == what:
+            return
+
+
+def backward_kept(rows, width, units):
+    tokens = BLOCKS * rows
+    return dict(
+        df=Out((BLOCKS, rows, width), BF16, True),
+        dgu=Out((2 * units, tokens), BF16, True),
+        a=Out((rows, width), BF16, True),
+        da=Out((rows, width), BF16, True),
+        dq=Out((rows, QUERY_COLUMNS), BF16, True),
+        dkv=Out((rows, 2 * KEY_COLUMNS), BF16, True),
+        gain=Out((1, 2 * width + 2 * HEAD_SIZE), F32, True),
+    )
+
+
+def backward_scratch(rows, width, units):
+    past = held_like(forward_kept(rows, width, units))
+    return held_like(backward_kept(rows, width, units)) | dict(
+        u=past["u"],
+        qraw=past["qraw"],
+        kraw=past["kraw"],
+        q=past["q"],
+        dh=pltpu.VMEM((rows, width), F32),
+        dx=pltpu.VMEM((rows, width), F32),
+        do5=pltpu.VMEM((QUERY_HEADS * rows, HEAD_SIZE), BF16),
+        dq5=pltpu.VMEM((QUERY_HEADS * rows, HEAD_SIZE), F32),
+        dkv_own=pltpu.VMEM((rows, 2 * KEY_COLUMNS), F32),
+        part=pltpu.VMEM((BLOCKS, rows, width), BF16),
+        land=pltpu.VMEM((BLOCKS - 1, rows, width), BF16),
+        part_kv=pltpu.VMEM((2 * BLOCKS, rows, 2 * KEY_COLUMNS), BF16),
+        sib_kv=pltpu.VMEM((BLOCKS, rows, 2 * KEY_COLUMNS), BF16),
+        land_kv=pltpu.VMEM((BLOCKS - 1, rows, 2 * KEY_COLUMNS), BF16),
+        df_sems=pair(21),
+        de_sems=pair(21),
+        kv_sems=pair(29),
+        held=pltpu.SemaphoreType.DMA((7,)),
+    )
+
+
+class BackwardLayer:
+    def __init__(self, r, place, m, need, past, source, kv_pieces=(KV_WIDTHS, CYCLES)):
+        self.r, self.place, self.m, self.need, self.kv_pieces = r, place, m, need, kv_pieces
+        self.past, self.source = past, source
+
+    def targets(self):
+        r = self.r
+        return dict(u=r.u, h=r.dh, qraw=r.qraw, kraw=r.kraw, q=r.q, kv=r.part_kv)
+
+    def _fetch(self, targets, start):
+        for section, past in enumerate(self.past):
+            if past is not None:
+
+                @pl.when(self.place.section == section)
+                def _(past=past):
+                    for i, (name, target) in enumerate(targets.items()):
+                        load(past[name], target, self.r.held.at[start + i])
+
+    def fetch(self):
+        self._fetch(self.targets(), 0)
+
+    def fetch_gu(self, gu):
+        self._fetch(dict(gu=gu), 6)
+
+    def rows_out(self):
+        r, place = self.r, self.place
+        first, second = self.source
+        if first is None:
+            dy = second[...]
+        elif second is None:
+            dy = first[...]
+        else:
+            dy = jnp.where(place.section == 0, first[...], second[...])
+        r.df[place.chip()] = dy
+        self.gather = Gather(place, r.df, column_pieces(ROW_WIDTHS, CYCLES), r.df_sems, False)
+        self.gather.start()
+
+        def put(index, total):
+            r.dx[index] = total
+
+        self.scatter = Scatter(place, r.get("part"), r.land, column_pieces(ROW_WIDTHS, CYCLES), r.de_sems, put)
+
+    def chunk(self, gu, flip):
+        r, place = self.r, self.place
+        rows, width = r.u.shape
+        units = r.dgu.shape[0] // 2
+        first = place.chip(flip) // 4 * 4
+        tokens = pl.ds(pl.multiple_of(first * rows, 4 * rows), 4 * rows)
+        here = pl.ds(first, 4)
+        for some in unit_blocks(units):
+            beyond = pl.ds(units + some.start, some.size)
+            dhidden = dot_nt(r.w.ffn[2, some], r.df[here].reshape(4 * rows, width))
+            gate, up = gu[some, tokens], gu[beyond, tokens]
+            shut = jax.nn.sigmoid(gate)
+            r.dgu[some, tokens] = (dhidden * up * (shut * (1.0 + gate * (1.0 - shut)))).astype(BF16)
+            r.dgu[beyond, tokens] = (dhidden * (gate * shut)).astype(BF16)
+        for some in column_blocks(width):
+            inward = dot_tn(r.dgu[:, tokens], r.w.ffn[:2, :, some].reshape(2 * units, some.size))
+            r.part[here, :, some] = inward.astype(BF16).reshape(4, rows, some.size)
+
+    def send(self, flip):
+        self.scatter.start([flip ^ mask for mask in (0, X_BIT, Y_BIT, X_BIT | Y_BIT)])
+
+    def feed_forward(self):
+        def inner(gu):
+            self.fetch_gu(gu)
+            self.need("ffn")
+            self.gather.finish()
+            landed(gu, self.r.held.at[6])
+            for flip in (Z_BIT, 0):
+                self.chunk(gu, flip)
+                self.send(flip)
+
+        units, tokens = self.r.dgu.shape
+        pl.run_scoped(inner, pltpu.VMEM((units, tokens), F32))
+
+    def steps(self, gu):
+        self.rows_out()
+        yield
+        self.gather.first()
+        yield
+        self.gather.second()
+        yield
+        self.need("ffn")
+        self.gather.third()
+        landed(gu, self.r.held.at[6])
+        self.chunk(gu, Z_BIT)
+        yield
+        self.send(Z_BIT)
+        yield
+        self.chunk(gu, 0)
+        yield
+        self.send(0)
+        yield
+        self.scatter.second()
+        yield
+        self.scatter.third()
+        yield
+        self.scatter.last()
+        self.middle()
+        yield
+        self.mixture()
+        yield
+        self.weights()
+        yield
+        self.key_siblings()
+        yield
+        self.queries()
+        yield
+        self.scatter_kv.second()
+        yield
+        self.scatter_kv.third()
+        yield
+        self.keys()
+        yield "result"
+
+    def middle(self):
+        r = self.r
+        rows, width = r.u.shape
+        ffn_gain = gain_parts(r, width)[1]
+        for i, target in enumerate(self.targets().values()):
+            landed(target, r.held.at[i])
+        unit, inverse = unit_rows(r.dh[...])
+        r.gain[:, width : 2 * width] = jnp.sum(r.dx[...] * unit, axis=0, keepdims=True)
+        r.dh[...] = r.df[self.place.chip()].astype(F32) + unit_back(r.dx[...] * ffn_gain, unit, inverse)
+        r.da[...] = r.dh[...].astype(BF16)
+        unit, _ = unit_rows(r.u[...].astype(F32))
+        r.a[...] = (unit * gain_parts(r, width)[0]).astype(BF16)
+
+    def attention(self):
+        self.mixture()
+        self.weights()
+        self.key_siblings()
+
+    def mixture(self):
+        r = self.r
+        rows, width = r.u.shape
+        self.need("out")
+        heads = QUERY_HEADS // 2
+        for t in range(2):
+            total = jnp.zeros((rows, HALF_COLUMNS), F32)
+            for c in range(8):
+                total = total + dot_nt(r.da[:, c * (width // 8) : (c + 1) * (width // 8)], r.w.out[t * 8 + c])
+            r.do5[t * heads * rows : (t + 1) * heads * rows] = stack_heads(total.astype(BF16), heads)
+
+    def weights(self):
+        r, m = self.r, self.m
+        rows = r.u.shape[0]
+        keys = 2 * BLOCKS * rows
+
+        def inner(q5, k5, v5, bias):
+            mask_bias(m, r, bias)
+            q5[...] = stack_heads(r.q[...], QUERY_HEADS).reshape(KEY_VALUE_HEADS, GROUP * rows, HEAD_SIZE)
+            split_keys(r.part_kv, k5, v5)
+
+            def attend(g, _):
+                at = pl.ds(pl.multiple_of(g * GROUP * rows, GROUP * rows), GROUP * rows)
+                weights = probabilities(q5[g], k5[g], bias[...])
+                grads = r.do5[at]
+                dweights = dot_nt(grads, v5[g])
+                mean = jnp.sum(weights * dweights, axis=-1, keepdims=True)
+                dscores = (weights * (dweights - mean)).astype(BF16)
+                r.dq5[at] = dot(dscores, k5[g])
+                k5[g] = dot_tn(dscores, q5[g]).astype(BF16)
+                v5[g] = dot_tn(weights.astype(BF16), grads).astype(BF16)
+                return 0
+
+            lax.fori_loop(0, KEY_VALUE_HEADS, attend, 0)
+            for b in range(2 * BLOCKS):
+                at = slice(b * rows, (b + 1) * rows)
+                r.part_kv[b] = jnp.concatenate(
+                    [k5[g, at] for g in range(KEY_VALUE_HEADS)] + [v5[g, at] for g in range(KEY_VALUE_HEADS)], axis=1
+                )
+
+        kind = pltpu.VMEM((KEY_VALUE_HEADS, keys, HEAD_SIZE), BF16)
+        grouped = pltpu.VMEM((KEY_VALUE_HEADS, GROUP * rows, HEAD_SIZE), BF16)
+        pl.run_scoped(inner, grouped, kind, kind, pltpu.VMEM((rows, keys), F32))
+
+    def key_siblings(self):
+        r, place = self.r, self.place
+
+        def put(index, total):
+            r.dkv_own[index] = total
+
+        pieces = column_pieces(*self.kv_pieces)
+        self.scatter_kv = Scatter(place, r.part_kv, r.land_kv, pieces, r.kv_sems, put, r.sib_kv)
+        self.scatter_kv.siblings()
+        self.scatter_kv.start()
+
+    def queries(self):
+        r, m = self.r, self.m
+        width = r.u.shape[1]
+        q_gain = gain_parts(r, width)[2]
+        cos, sin = r.rowtab[m, :, :HEAD_SIZE], r.rowtab[m, :, HEAD_SIZE : 2 * HEAD_SIZE]
+        unit, inverse = unit_rows(stack_heads(r.qraw[...], QUERY_HEADS))
+        dhat = unrope(r.dq5[...] * SCALE, cos, sin, QUERY_HEADS)
+        r.gain[:, 2 * width : 2 * width + HEAD_SIZE] = jnp.sum(dhat * unit, axis=0, keepdims=True)
+        r.dq[...] = spread_heads(unit_back(dhat * q_gain, unit, inverse), QUERY_HEADS).astype(BF16)
+        self.need("query")
+        r.dx[...] = dot_nt(r.dq[:, :HALF_COLUMNS], r.w.query[:8].reshape(width, HALF_COLUMNS)) + dot_nt(
+            r.dq[:, HALF_COLUMNS:], r.w.query[8:].reshape(width, HALF_COLUMNS)
+        )
+
+    def key_sums(self):
+        self.scatter_kv.second()
+        self.scatter_kv.third()
+
+    def keys(self):
+        r, m = self.r, self.m
+        width = r.u.shape[1]
+        attn_gain, _, _, k_gain = gain_parts(r, width)
+        cos, sin = r.rowtab[m, :, :HEAD_SIZE], r.rowtab[m, :, HEAD_SIZE : 2 * HEAD_SIZE]
+        self.need("keyval")
+        self.scatter_kv.last()
+        unit, inverse = unit_rows(stack_heads(r.kraw[:, :KEY_COLUMNS], KEY_VALUE_HEADS))
+        dhat = unrope(stack_heads(r.dkv_own[:, :KEY_COLUMNS], KEY_VALUE_HEADS), cos, sin, KEY_VALUE_HEADS)
+        r.gain[:, 2 * width + HEAD_SIZE :] = jnp.sum(dhat * unit, axis=0, keepdims=True)
+        dk_raw = spread_heads(unit_back(dhat * k_gain, unit, inverse), KEY_VALUE_HEADS)
+        r.dkv[...] = jnp.concatenate([dk_raw, r.dkv_own[:, KEY_COLUMNS:]], axis=1).astype(BF16)
+        r.dx[...] = r.dx[...] + dot_nt(r.dkv[...], r.w.keyval[...].reshape(width, 2 * KEY_COLUMNS))
+        unit, inverse = unit_rows(r.u[...].astype(F32))
+        r.gain[:, :width] = jnp.sum(r.dx[...] * unit, axis=0, keepdims=True)
+        r.grad[...] = (r.dh[...] + unit_back(r.dx[...] * attn_gain, unit, inverse)).astype(BF16)
+
+    def drain(self):
+        for sent in (self.gather, self.scatter, self.scatter_kv):
+            sent.drain()
+
+
+WEIGHTS = ("keyval", "query", "out", "ffn")
+SCHEDULE = "bbbsbbbbrfbfbfbfbfbfbffbffbbbofff"
+NEIGHBOURS = (C_BIT, X_BIT, Y_BIT, Z_BIT)
+AWAY = (X_BIT | Y_BIT, X_BIT, Y_BIT)
+
+
+class Arrival:
+    def __init__(self, place, i, s, store):
+        self.place, self.i, self.s, self.store = place, i, s, store
+        self.columns = i.down.shape[1]
+        self.units = s.w.ffn.shape[1]
+        own = place.block()
+        self.fetched = [
+            load(src, dst, s.fetch.at[n])
+            for n, (src, dst) in enumerate(
+                (
+                    (i.gains, s.gains_all.at[own]),
+                    (i.keyval, s.w.keyval.at[own]),
+                    (i.query, s.w.query.at[own]),
+                    (i.out, s.w.out.at[own]),
+                    (i.gateup.at[:, self._units(0), :], s.w.ffn.at[pl.ds(0, 2), :, self._columns(0)]),
+                    (i.down.at[self._units(0), :], s.w.ffn.at[2, :, self._columns(0)]),
+                )
+            )
+        ]
+        self.gains = Gather(place, s.gains_all, row_pieces((16,), TOWARD_Z), s.gains_sems, True)
+        self.keyval, self.query, self.out = (
+            Gather(place, buf, halves(buf.shape[1]), pair_, True)
+            for buf, pair_ in (
+                (s.w.keyval, s.keyval_sems),
+                (s.w.query, s.query_sems),
+                (s.w.out, s.out_sems),
+            )
+        )
+
+    def _units(self, mask):
+        return pl.ds(pl.multiple_of((self.place.chip(mask) % 4) * self.units, self.units), self.units)
+
+    def _columns(self, mask):
+        return pl.ds(pl.multiple_of(self.place.ctx(mask) * self.columns, self.columns), self.columns)
+
+    def _spread(self, mask, j):
+        i, s, mine = self.i, self.s, self._columns(0)
+        src, dst = (
+            (i.gateup.at[:, self._units(mask), :], s.w.ffn.at[pl.ds(0, 2), :, mine]),
+            (i.down.at[self._units(mask), :], s.w.ffn.at[2, :, mine]),
+        )[j]
+        return remote(src, dst, s.ffn_send.at[mask + j], s.ffn_recv.at[mask + j], self.place.peer(mask))
+
+    def _came(self, mask, j):
+        s, there = self.s, self._columns(mask)
+        dst = s.w.ffn.at[2, :, there] if j else s.w.ffn.at[pl.ds(0, 2), :, there]
+        remote(dst, dst, s.ffn_send.at[mask + j], s.ffn_recv.at[mask + j], self.place.peer(mask)).wait_recv()
+
+    def _sibling(self, mask, back=0):
+        s = self.s
+        where = s.w.ffn.at[:, :, self._columns(mask | back)]
+        slot = 8 + mask // 2
+        return remote(where, where, s.ffn_send.at[slot], s.ffn_recv.at[slot], self.place.peer(C_BIT))
+
+    def spread(self, masks):
+        for mask in masks:
+            for j in (0, 1):
+                self._spread(mask, j).start()
+
+    def begin(self):
+        for n, gather in enumerate((self.gains, self.keyval, self.query)):
+            self.fetched[n].wait()
+            gather.start()
+        for n in (3, 4, 5):
+            self.fetched[n].wait()
+        self._sibling(0).start()
+        for gather in (self.gains, self.keyval, self.query):
+            gather.first()
+        for gather in (self.gains, self.keyval, self.query):
+            gather.second()
+        self.out.start()
+        self.spread((X_BIT | Y_BIT,))
+        self.gains.third()
+        self.gains.last()
+
+    def keys_moving(self, phase):
+        if phase == 0:
+            self.out.first()
+        if phase == 1:
+            self.out.second()
+            self.spread((X_BIT, Y_BIT))
+
+    def need(self, name):
+        if name == "keyval":
+            self.keyval.third()
+            self.keyval.last()
+        if name == "query":
+            self.query.third()
+            self.query.last()
+        if name == "out":
+            self.out.third()
+            self.out.last()
+        if name == "ffn":
+            for mask in AWAY:
+                for j in (0, 1):
+                    self._came(mask, j)
+                self._sibling(mask).start()
+            for mask in (0,) + AWAY:
+                self._sibling(mask, C_BIT).wait_recv()
+        n = WEIGHTS.index(name)
+        load(self.s.w[name], self.store[name], self.s.store.at[n])
+
+    def drain(self):
+        for gather in (self.gains, self.keyval, self.query, self.out):
+            gather.drain()
+        for mask in AWAY:
+            for j in (0, 1):
+                self._spread(mask, j).wait_send()
+        for mask in (0,) + AWAY:
+            self._sibling(mask).wait_send()
+        for n, name in enumerate(WEIGHTS):
+            landed(self.store[name], self.s.store.at[n])
+
+
+def most_layers(inputs, cotangent, shards, tables):
+    rows, width = inputs.shape[1:]
+    units = shards["down"].shape[0] // 4
+    entries = 2 * width + 2 * HEAD_SIZE
+    share = entries // 16
+    steps = inputs.shape[0] + 1
+    shapes = dict(zip(WEIGHTS, [(16,) + shards[name].shape for name in WEIGHTS[:3]] + [(3, units, width)]))
+    own = (rows, width)
+
+    def body(i, o, s):
+        place = Place()
+        arrival = Arrival(place, i.shards, s, o.weights)
+        greet(place, NEIGHBOURS + (X_BIT | Y_BIT,), into="both")
+        arrival.begin()
+        s.gains[...] = jnp.concatenate([s.gains_all[n, 0:1, :share].astype(F32) for n in range(16)], axis=1)
+
+        def ahead(step, need):
+            m = jnp.clip(step - place.section, 0, inputs.shape[0] - 1)
+            r = Refs(
+                s.f | i.tables,
+                w=s.w,
+                gains=s.gains,
+                inputs=i.inputs,
+                received=None if step == 0 else s.received.at[step - 1],
+                result=s.result.at[step],
+                kept=o.fwd[step],
+            )
+            return forward_steps(r, place, m, need)
+
+        def back(step, m, past, source):
+            r = Refs(s.b | i.tables, w=s.w, gains=s.gains, grad=s.grad.at[step])
+            return BackwardLayer(r, place, m, lambda name: None, past, source)
+
+        def save_back(step):
+            return [load(s.b[name], o.back[step][name], s.keep.at[n]) for n, name in enumerate(o.back[step])]
+
+        def publish(sources, target, slots, section):
+            @pl.when(place.section == section)
+            def _():
+                for n, (source, slot) in enumerate(zip(sources, slots)):
+                    load(source, target.at[slot], s.publish.at[n])
+                for n, (source, slot) in enumerate(zip(sources, slots)):
+                    landed(target.at[slot], s.publish.at[n])
+
+        def courier(source, target, n, into):
+            return Courier(place, source, target, (s.pass_send.at[n], s.pass_recv.at[n]), into)
+
+        def tell(n):
+            for mask in NEIGHBOURS:
+                pl.semaphore_signal(s.steps.at[n], inc=1, device_id=place.peer(mask), device_id_type=MESH_ID)
+
+        def hear(n):
+            pl.semaphore_wait(s.steps.at[n], len(NEIGHBOURS))
+
+        first = ahead(0, arrival.need)
+        take(first, 1)
+        for phase in (0, 1):
+            take(first, 1)
+            arrival.keys_moving(phase)
+        until(first, "result")
+        passes = [courier(s.result.at[0], s.received.at[0], 0, 1)]
+        passes[0].start()
+        until(first, None)
+        tell(0)
+        store_gains = load(s.gains, o.gains, s.store.at[4])
+
+        passes[0].arrive()
+        hear(0)
+        second = ahead(1, lambda name: None)
+        until(second, "result")
+        passes.append(courier(s.result.at[1], s.received.at[1], 1, 1))
+        until(second, None)
+        tell(1)
+        hear(1)
+
+        layer = back(0, 0, (o.fwd[1], o.fwd[1]), (None, i.cotangent.at[0]))
+        layer.fetch()
+        layer.fetch_gu(s.gu_back)
+        passes.append(courier(s.grad.at[0], s.returned, 2, 0))
+        one, other = layer.steps(s.gu_back), ahead(2, lambda name: None)
+        for turn in SCHEDULE:
+            if turn == "s":
+                passes[1].start()
+            elif turn == "r":
+                passes[1].arrive()
+            elif turn == "o":
+                passes[2].start()
+                saves = save_back(0)
+            else:
+                take(one if turn == "b" else other, 1)
+        until(one, None)
+        until(other, None)
+        layer.drain()
+        for copy in saves:
+            copy.wait()
+        tell(2)
+
+        layer = back(1, place.section, (o.fwd[0], o.fwd[2]), (s.returned, i.cotangent.at[1]))
+        layer.fetch()
+        layer.fetch_gu(s.gu_back)
+        passes[2].arrive()
+        hear(2)
+        until(layer.steps(s.gu_back), "result")
+        passes.append(courier(s.grad.at[1], o.passed, 3, 0))
+        passes[3].start()
+        saves = save_back(1)
+        publish([s.result.at[0], s.result.at[1]], o.section, (0, 1), 0)
+        publish([s.result.at[1], s.result.at[2]], o.section, (0, 1), 1)
+        publish([s.grad.at[1]], o.grads, (0,), 0)
+        publish([s.grad.at[0], s.grad.at[1]], o.grads, (0, 1), 1)
+        layer.drain()
+        arrival.drain()
+        store_gains.wait()
+        for copy in saves:
+            copy.wait()
+        passes[3].arrive()
+        for taken in passes:
+            taken.leave()
+
+    outputs = dict(
+        section=Out((2,) + own, BF16, True),
+        grads=Out((2,) + own, BF16, True),
+        passed=Out(own, BF16, True),
+        weights={name: Out(shape, BF16, True) for name, shape in shapes.items()},
+        gains=Out((1, entries), F32, True),
+        fwd=[forward_kept(rows, width, units) for _ in range(steps)],
+        back=[backward_kept(rows, width, units) for _ in range(steps - 1)],
+    )
+    scratch = dict(
+        f=forward_scratch(rows, width, units),
+        b=backward_scratch(rows, width, units),
+        w={name: pltpu.VMEM(shape, BF16) for name, shape in shapes.items()},
+        gains=pltpu.VMEM((1, entries), F32),
+        gains_all=pltpu.VMEM((16,) + shards["gains"].shape, BF16),
+        gu_back=pltpu.VMEM((2 * units, BLOCKS * rows), F32),
+        result=pltpu.VMEM((steps,) + own, BF16),
+        grad=pltpu.VMEM((steps - 1,) + own, BF16),
+        received=pltpu.VMEM((steps - 1,) + own, BF16),
+        returned=pltpu.VMEM(own, BF16),
+        gains_sems=pair(15),
+        keyval_sems=pair(30),
+        query_sems=pair(30),
+        out_sems=pair(30),
+        ffn_send=pltpu.SemaphoreType.DMA((12,)),
+        ffn_recv=pltpu.SemaphoreType.DMA((12,)),
+        fetch=pltpu.SemaphoreType.DMA((6,)),
+        store=pltpu.SemaphoreType.DMA((5,)),
+        keep=pltpu.SemaphoreType.DMA((7,)),
+        publish=pltpu.SemaphoreType.DMA((2,)),
+        pass_send=pltpu.SemaphoreType.DMA((4,)),
+        pass_recv=pltpu.SemaphoreType.DMA((4,)),
+        steps=pltpu.SemaphoreType.REGULAR((3,)),
+    )
+    operands = near(inputs=inputs, cotangent=cotangent) | dict(tables=near(**tables), shards=far(**shards))
+    return run(body, 0, operands, outputs, scratch)
+
+
+GRAD_ROWS = ("a", "da", "ob", "dq", "dkv")
+
+
+def last_layer(returned, grads, weights, gains, tables, past, kept):
+    rows, width = returned.shape
+    units = weights["ffn"].shape[1]
+    tokens = BLOCKS * rows
+    columns = width // 8
+    entries = 2 * width + 2 * HEAD_SIZE
+    last = len(kept[0]) - 1
+    parts = dict(query=(columns, HALF_COLUMNS), keyval=(width // 16, 2 * KEY_COLUMNS), out=(HALF_COLUMNS, columns))
+    lines = -(-entries // 1024) * 8
+
+    def body(i, o, s):
+        place = Place()
+        core = place.bits[0]
+
+        def on(section):
+            return pl.when(place.section == section)
+
+        r = Refs(
+            s.b | {name: s.x[name].at[0, last] for name in ("a", "da", "dq", "dkv")} | i.tables,
+            w=dict(s.w),
+            gains=i.gains,
+            grad=o.grads.at[last],
+        )
+        r["w"] = Refs(s.w)
+        layer = BackwardLayer(
+            r, place, last, lambda name: None, (i.past, None), (i.returned, None), ((384, 256), TOWARD_Z)
+        )
+        greet(place, NEIGHBOURS + (X_BIT | Y_BIT,))
+
+        @on(0)
+        def _():
+            layer.rows_out()
+            layer.fetch()
+            load(i.grads.at[0], o.grads.at[0], s.turn.at[0])
+
+        @on(1)
+        def _():
+            for m in range(2):
+                load(i.grads.at[m], o.grads.at[m], s.turn.at[m])
+            load(i.kept[1][1].df, r.df, r.held.at[0])
+            load(i.kept[1][1].dgu, r.dgu, r.held.at[1])
+
+        loads = {name: load(i.weights[name], s.w[name], s.fetch.at[n]) for n, name in enumerate(s.w)}
+
+        def own_rows(start):
+            for n, name in enumerate(GRAD_ROWS):
+                for m in range(2):
+                    for section in (0, 1):
+                        if name in i.kept[section][m]:
+
+                            @on(section)
+                            def _():
+                                source, target = i.kept[section][m][name], s.x[name].at[0, m]
+                                if start:
+                                    load(source, target, s.rows.at[2 * n + m])
+                                else:
+                                    landed(target, s.rows.at[2 * n + m])
+
+        own_rows(True)
+        for section in (0, 1):
+
+            @on(section)
+            def _():
+                load(i.kept[section][0].gain, s.gain_kept, s.rows.at[10])
+                if section == 1:
+                    load(i.kept[1][1].gain, r.gain, s.rows.at[11])
+
+        def exchange(name, m):
+            n = 2 * GRAD_ROWS.index(name) + m
+            buf = s.x[name]
+            return remote(buf.at[0, m], buf.at[1, m], s.x_send.at[n], s.x_recv.at[n], place.peer(C_BIT))
+
+        loads["ffn"].wait()
+
+        def at(mask):
+            return pl.ds(pl.multiple_of(place.ctx(mask) * columns, columns), columns)
+
+        def units_at(mask):
+            return pl.ds(pl.multiple_of((place.chip(mask) % 4) * units, units), units)
+
+        def to_sibling(n, mask):
+            where = s.w.ffn.at[:, :, at(mask | C_BIT)]
+            return remote(where, s.sib_ffn.at[n], s.sib_send.at[n], s.sib_recv.at[n], place.peer(C_BIT))
+
+        def to_owner(mask):
+            n = mask // 2
+            source, target = s.w.ffn.at[:, :, at(mask)], o.ffn.at[:, units_at(0), :]
+            return remote(source, target, s.ffn_send.at[n], s.ffn_recv.at[n], place.peer(mask))
+
+        def from_owner(mask):
+            n = mask // 2
+            where = o.ffn.at[:, units_at(mask), :]
+            remote(where, where, s.ffn_send.at[n], s.ffn_recv.at[n], place.peer(mask)).wait_recv()
+
+        def ffn_grads(e, hid, df_0, dgu_0):
+            for section in (0, 1):
+
+                @on(section)
+                def _():
+                    for m, kept_m in enumerate(i.kept[section]):
+                        load(kept_m.e, e.at[m], s.wide.at[m])
+                        load(kept_m.hid, hid.at[m], s.wide.at[2 + m])
+                    load(i.kept[section][0].df, df_0, s.wide.at[4])
+                    load(i.kept[section][0].dgu, dgu_0, s.wide.at[5])
+
+            @on(1)
+            def _():
+                landed(r.df, r.held.at[0])
+                landed(r.dgu, r.held.at[1])
+
+            for m in range(2):
+                landed(e.at[m], s.wide.at[m])
+                landed(hid.at[m], s.wide.at[2 + m])
+            landed(df_0, s.wide.at[4])
+            landed(dgu_0, s.wide.at[5])
+
+            def partial(mask):
+                where = at(mask)
+                up = jnp.zeros((2 * units, columns), F32)
+                down = jnp.zeros((units, columns), F32)
+                for m, (dgu, df) in enumerate(((dgu_0, df_0), (r.dgu, r.df))):
+                    up = up + dot(dgu[...], e[m, :, :, where].reshape(tokens, columns))
+                    down = down + dot(hid[m], df[:, :, where].reshape(tokens, columns))
+                return up, down
+
+            def store(mask, up, down):
+                s.w.ffn[:2, :, at(mask)] = up.astype(BF16).reshape(2, units, columns)
+                s.w.ffn[2, :, at(mask)] = down.astype(BF16)
+
+            for n, mask in enumerate(AWAY + (0,)):
+                store(mask | C_BIT, *partial(mask | C_BIT))
+                to_sibling(n, mask).start()
+
+            @on(0)
+            def _():
+                layer.scatter.second()
+
+            for n, mask in enumerate(AWAY + (0,)):
+                up, down = partial(mask)
+                to_sibling(n, mask).wait_recv()
+                up = up + s.sib_ffn[n, :2].astype(F32).reshape(2 * units, columns)
+                store(mask, up, down + s.sib_ffn[n, 2].astype(F32))
+                if n == 2:
+
+                    @on(0)
+                    def _():
+                        layer.scatter.third()
+
+            to_owner(X_BIT | Y_BIT).start()
+            load(s.w.ffn.at[:, :, at(0)], o.ffn.at[:, units_at(0), :], s.fetch.at[4])
+
+            @on(0)
+            def _():
+                layer.scatter.last()
+
+        def front(part):
+            r["part"] = part
+
+            @on(0)
+            def _():
+                layer.scatter.part = part
+                layer.feed_forward()
+
+            pl.run_scoped(
+                ffn_grads,
+                pltpu.VMEM((2, BLOCKS, rows, width), BF16),
+                pltpu.VMEM((2, units, tokens), BF16),
+                pltpu.VMEM((BLOCKS, rows, width), BF16),
+                pltpu.VMEM((2 * units, tokens), BF16),
+            )
+
+            @on(0)
+            def _():
+                layer.scatter.drain()
+
+        pl.run_scoped(front, pltpu.VMEM((BLOCKS, rows, width), BF16))
+
+        @on(0)
+        def _():
+            layer.middle()
+
+        own_rows(False)
+
+        def swap(names, ms):
+            for name in names:
+                for m in ms:
+                    exchange(name, m).start()
+
+        swap(("ob", "da", "a"), (0, 1))
+        swap(("dq", "dkv"), (0,))
+
+        def both(name, where):
+            return s.x[name][:, :, :, where].reshape(4 * rows, where.size)
+
+        def got(names, ms):
+            for name in names:
+                for m in ms:
+                    exchange(name, m).wait_recv()
+
+        def putter(ref):
+            def put(index, total):
+                ref[index] = total
+
+            return put
+
+        scatters = Refs()
+        for name in parts:
+            pieces = row_pieces((48, 48, 32), CYCLES) if name == "keyval" else halves(parts[name][0])
+            scatters[name] = Scatter(place, s.part[name], s.land[name], pieces, s.sums[name], putter(o.attention[name]))
+
+        def wide_columns(c):
+            return pl.ds(pl.multiple_of((2 * c + core) * columns, columns), columns)
+
+        def half(z):
+            return pl.ds(z * HALF_COLUMNS, HALF_COLUMNS)
+
+        got(("ob", "da"), (0, 1))
+        for z in (0, 1):
+            for c in range(4):
+                s.part.out[4 * z + c] = dot_tn(both("ob", half(z)), both("da", wide_columns(c))).astype(BF16)
+        scatters.out.start(pieces=(0,))
+
+        def rest(w_keyval, w_query, do5, dq5):
+            r.update(do5=do5, dq5=dq5)
+            r.w.update(keyval=w_keyval, query=w_query)
+            load(i.weights.keyval, w_keyval, s.fetch.at[3])
+            load(i.weights.query, w_query, s.fetch.at[2])
+            loads["out"].wait()
+
+            @on(0)
+            def _():
+                layer.attention()
+
+            scatters.out.start(pieces=(1,))
+            landed(w_query, s.fetch.at[2])
+            landed(w_keyval, s.fetch.at[3])
+
+            @on(0)
+            def _():
+                layer.queries()
+
+            swap(("dq",), (1,))
+            got(("a", "dq"), (0, 1))
+            for z in (0, 1):
+                for c in range(4):
+                    s.part.query[4 * z + c] = dot_tn(both("a", wide_columns(c)), both("dq", half(z))).astype(BF16)
+            scatters.query.start()
+
+            @on(0)
+            def _():
+                layer.key_sums()
+
+            to_owner(X_BIT).start()
+            to_owner(Y_BIT).start()
+
+            @on(0)
+            def _():
+                layer.keys()
+
+            swap(("dkv",), (1,))
+
+        pl.run_scoped(
+            rest,
+            pltpu.VMEM(weights["keyval"].shape, BF16),
+            pltpu.VMEM(weights["query"].shape, BF16),
+            pltpu.VMEM((QUERY_HEADS * rows, HEAD_SIZE), BF16),
+            pltpu.VMEM((QUERY_HEADS * rows, HEAD_SIZE), F32),
+        )
+        got(("dkv",), (0, 1))
+        narrow = width // 16
+        for z in (0, 1):
+            for c in range(4):
+                where = pl.ds(pl.multiple_of((8 * z + 2 * c + core) * narrow, narrow), narrow)
+                every = pl.ds(0, 2 * KEY_COLUMNS)
+                s.part.keyval[4 * z + c] = dot_tn(both("a", where), both("dkv", every)).astype(BF16)
+        scatters.keyval.start()
+
+        landed(s.gain_kept, s.rows.at[10])
+
+        @on(1)
+        def _():
+            landed(r.gain, s.rows.at[11])
+
+        total = s.gain_kept[...] + r.gain[...]
+        lanes = entries // 128
+        padding = jnp.zeros((lines - lanes, 128), F32)
+        s.gain_all[place.block()] = jnp.concatenate(
+            [total[:, n * 128 : (n + 1) * 128] for n in range(lanes)] + [padding], axis=0
+        )
+        gain_gather = Gather(place, s.gain_all, row_pieces((lines,), TOWARD_Z), s.gain_sems, True)
+        gain_gather.start()
+        scatters.out.second()
+        gain_gather.first()
+        gain_gather.second()
+        scatters.query.second()
+        scatters.out.third()
+        scatters.keyval.second()
+        scatters.query.third()
+        scatters.out.last()
+        scatters.keyval.third()
+        gain_gather.third()
+        scatters.query.last()
+        scatters.keyval.last()
+        gain_gather.last()
+        total = s.gain_all[0]
+        for n in range(1, 16):
+            total = total + s.gain_all[n]
+        o.gains[...] = total
+        for mask in AWAY:
+            from_owner(mask)
+        for mask in AWAY:
+            to_owner(mask).wait_send()
+        landed(o.ffn.at[:, units_at(0), :], s.fetch.at[4])
+        for n, mask in enumerate(AWAY + (0,)):
+            to_sibling(n, mask).wait_send()
+        for name in GRAD_ROWS:
+            for m in range(2):
+                exchange(name, m).wait_send()
+        for scatter in scatters.values():
+            scatter.drain()
+        gain_gather.drain()
+        landed(o.grads.at[0], s.turn.at[0])
+
+        @on(0)
+        def _():
+            layer.gather.drain()
+            layer.scatter_kv.drain()
+
+        @on(1)
+        def _():
+            landed(o.grads.at[1], s.turn.at[1])
+
+    outputs = dict(
+        grads=Out((2, rows, width), BF16, False),
+        attention={name: Out(shape, F32, False) for name, shape in parts.items()},
+        ffn=Out((3, 4 * units, columns), BF16, True),
+        gains=Out((lines, 128), F32, False),
+    )
+    b = backward_scratch(rows, width, units)
+    row_widths = dict(zip(GRAD_ROWS, (width, width, QUERY_COLUMNS, QUERY_COLUMNS, 2 * KEY_COLUMNS)))
+    for name in ("a", "da", "dq", "dkv", "do5", "dq5", "part"):
+        del b[name]
+    scratch = dict(
+        b=b,
+        w={name: pltpu.VMEM(weights[name].shape, BF16) for name in ("ffn", "out")},
+        gain_kept=pltpu.VMEM((1, entries), F32),
+        gain_all=pltpu.VMEM((16, lines, 128), F32),
+        sib_ffn=pltpu.VMEM((4, 3, units, columns), BF16),
+        x={name: pltpu.VMEM((2, 2, rows, size), BF16) for name, size in row_widths.items()},
+        part={name: pltpu.VMEM((BLOCKS,) + shape, BF16) for name, shape in parts.items()},
+        land={name: pltpu.VMEM((BLOCKS - 1,) + shape, BF16) for name, shape in parts.items()},
+        sums={name: pair(21) for name in parts},
+        gain_sems=pair(15),
+        ffn_send=pltpu.SemaphoreType.DMA((4,)),
+        ffn_recv=pltpu.SemaphoreType.DMA((4,)),
+        sib_send=pltpu.SemaphoreType.DMA((4,)),
+        sib_recv=pltpu.SemaphoreType.DMA((4,)),
+        x_send=pltpu.SemaphoreType.DMA((10,)),
+        x_recv=pltpu.SemaphoreType.DMA((10,)),
+        fetch=pltpu.SemaphoreType.DMA((5,)),
+        rows=pltpu.SemaphoreType.DMA((12,)),
+        wide=pltpu.SemaphoreType.DMA((6,)),
+        turn=pltpu.SemaphoreType.DMA((2,)),
+    )
+    operands = near(returned=returned, gains=gains) | far(grads=grads) | dict(tables=near(**tables))
+    operands |= dict(weights=far(**weights), past=far(**{name: past[name] for name in BACK_NEEDS}))
+    operands["kept"] = [[far(**{n: x for n, x in one.items() if n in GRAD_NEEDS}) for one in side] for side in kept]
+    return run(body, 1, operands, outputs, scratch)
+
+
+BACK_NEEDS = ("u", "h", "qraw", "kraw", "q", "kv", "gu")
+GRAD_NEEDS = ("e", "hid", "df", "dgu", "gain") + GRAD_ROWS
+
+
+def gradients_out(ffn):
+    units, columns = ffn.shape[1:]
+    steps = 4
+    some = units // steps
+
+    def body(source, gateup, down):
+        for j in range(2):
+            gateup[:, j, :] = jnp.transpose(source[j]).astype(F32)
+        down[...] = source[2].astype(F32)
+
+    return pl.pallas_call(
+        body,
+        grid=(steps,),
+        in_specs=[pl.BlockSpec((3, some, columns), lambda i: (0, i, 0))],
+        out_specs=(
+            pl.BlockSpec((columns, 2, some), lambda i: (0, 0, i)),
+            pl.BlockSpec((some, columns), lambda i: (i, 0)),
+        ),
+        out_shape=(
+            jax.ShapeDtypeStruct((columns, 2, units), F32),
+            jax.ShapeDtypeStruct((units, columns), F32),
+        ),
+        compiler_params=pltpu.CompilerParams(vmem_limit_bytes=VMEM_BYTES),
+    )(ffn)
+
+
+def cube_device(
+    inputs,
+    cotangent,
+    slot_order,
+    query_weight,
+    key_value_matrix,
+    out_weight,
+    gateup_weight,
+    down_weight,
+    norm_gains,
+):
+    tensor_id = lax.axis_index("tensor")
+    context_id = lax.axis_index("ctx")
+    batches, rows, width = inputs.shape
+    tensors, contexts = 2, 8
+    span = rows * tensors
+    share = norm_gains.shape[1]
+    shards = dict(
+        query=query_weight[0],
+        keyval=key_value_matrix[0],
+        out=out_weight[0],
+        gateup=jnp.transpose(gateup_weight[0], (1, 2, 0)),
+        down=down_weight[0],
+        gains=jnp.pad(norm_gains, ((0, 15), (0, -share % 128))),
+    )
+    own_slot = jnp.sum(jnp.where(jnp.arange(contexts) == context_id, slot_order, 0), axis=1)
+    own_pos = own_slot[:, None] * span + tensor_id * rows + jnp.arange(rows)[None, :]
+    half_width = HEAD_SIZE // 2
+    frequency = ROPE_BASE ** (-(jnp.arange(half_width, dtype=F32) * 2.0) / HEAD_SIZE)
+    angles = own_pos.astype(F32)[..., None] * frequency
+    cosine, sine = jnp.cos(angles), jnp.sin(angles)
+    rowtab = jnp.concatenate(
+        [cosine, cosine, -sine, sine, jnp.broadcast_to(own_pos.astype(F32)[..., None], (batches, rows, 128))], axis=-1
+    )
+    within = jnp.arange(tensors)[:, None, None] * rows + jnp.arange(rows)[None, None, :]
+    key_pos = (slot_order[:, None, :, None] * span + within[None]).reshape(batches, 1, -1)
+    tables = dict(rowtab=rowtab, postab=key_pos.astype(F32))
+    layers = most_layers(inputs, cotangent, shards, tables)
+    fwd, back = layers["fwd"], layers["back"]
+    kept = [[fwd[0] | back[1], fwd[1]], [fwd[1] | back[0], fwd[2] | back[1]]]
+    last = last_layer(layers["passed"], layers["grads"], layers["weights"], layers["gains"], tables, fwd[1], kept)
+    start = (tensor_id * contexts + context_id) * share
+    attention = last["attention"]
+    grad_gateup, grad_down = gradients_out(last["ffn"])
+    return (
+        layers["section"][None],
+        last["grads"][None],
+        attention["query"][None],
+        attention["keyval"][None],
+        attention["out"][None],
+        grad_gateup[None],
+        grad_down[None],
+        lax.dynamic_slice(last["gains"].reshape(-1), (start,), (share,))[None],
+    )
+
+
+def fits_cube(mesh):
+    return mesh.shape["section"] == 2 and mesh.shape["tensor"] == 2 and mesh.shape["ctx"] == 8
+
+
 def solution(mesh):
     return jax.shard_map(
-        per_device,
+        cube_device if fits_cube(mesh) else per_device,
         mesh=mesh,
         in_specs=(
             P(None, ("tensor", "ctx"), None),

time: 1690 us -> 519 us (0.31)
  waiting for transfers between devices: 846 us -> 0 us
  Pallas kernels: 0 us -> 496 us
  matrix products: 253 us -> 0 us
  blocking collectives: 223 us -> 0 us
  local copies, waits for them, and re-layouts: 203 us -> 15.1 us
  other arithmetic: 120 us -> 1.9 us
  between operations: 21.9 us -> 0.94 us
    pallas_call x0 -> x3, Pallas kernels: none -> 496 us  [the longest x2 490 us: run(): pl.pallas_call(kernel, out_shape=tuple((jax.ShapeDtypeStruct(leaf.shape,...]
    reduce_scatter x16 -> x0, waiting for transfers between devices: 309 us -> none  [the longest x12 113 us: scatter_rows(): lax.psum_scatter(values.astype(jnp.bfloat16), 'tensor', scatter_dimension...]
    unnamed x32 -> x0, waiting for transfers between devices: 308 us -> none
    dot_general x119 -> x0, matrix products: 253 us -> none  [the longest x5 36.4 us: row_product(): lax.dot_general(left_rows, right_rows, (((0,), (0,)), ((), ())), preferre...]
    all_gather x8 -> x0, waiting for transfers between devices: 189 us -> none  [the longest x1 96.9 us: per_device(): gateup_full = lax.all_gather(gateup_weight[0], 'ctx', axis=0, tiled=True)]
    all_gather x12 -> x0, blocking collectives: 114 us -> none  [gather_rows(): return lax.all_gather(values, 'tensor', axis=0, tiled=True)]
    unnamed x2 -> x0, blocking collectives: 109 us -> none
    unnamed x488 -> x16, local copies, waits for them, and re-layouts: 69.7 us -> 11.3 us
  transfers between devices with their start and end apart: 32 -> 0, of which waited for: 27 -> 0; matrix products, arithmetic and copies ran while one was open for 16% -> 0% of each run, Pallas kernels for 0% -> 0%
where the time goes in v2:
time: 519 us; the launch traced here: 514 us
  Pallas kernels  496 us (96%)
  local copies, waits for them, and re-layouts  15.1 us (3%)
    pallas_call x2, Pallas kernels, run(): pl.pallas_call(kernel, out_shape=tuple((jax.ShapeDtypeStruct(leaf.shape,...  490 us
    unnamed x16, local copies, waits for them, and re-layouts  11.3 us

profile of v2, /device:TPU:0, one launch (start us, length us, event | category | flops | bytes accessed | tf_op | source)
XLA Modules:
  0.0 514.4 jit_solution(6191079262667174135)
XLA Ops:
  0.7 0.1 iota_add_fusion
  0.7 0.8 select_reduce_fusion
  1.6 0.1 add_convert_fusion.1
  1.6 0.1 add.88
  1.7 1.3 pad.4.refs_3_
  3.0 0.1 add.82
  3.1 0.1 add.83
  3.1 0.6 add_convert_fusion.refs_8_.refs_43_
  3.8 0.1 broadcast_in_dim.48
  3.8 0.3 multiply_sine_fusion
  4.2 0.8 concatenate.3.refs_9_.refs_44_
  4.9 7.3 %copy.17 = bf16[1,256,2,2560]{1,3,2,0:T(8,128)(2,1)} copy(bf16[1,256,2,2560]{3,2,1,0:T(2,128)(2,1)} %param.15) | data formatting | bytes 5242880 | tf_op args[6]
  12.3 365.6 %shard_map.152 = (bf16[64,2048]{1,0:T(8,128)(2,1)}, bf16[64,2048]{1,0:T(8,128)(2,1)}, bf16[8,64,2048]{2,1,0:T(8,128)(2,1)}, bf16[1280,512]{1,0:T(8,128)(2,1)}, b...) custom-call(bf16[2,64,2048]{2,1,0:T(8,128)(2,1)} %refs_0_.1, ...), custom_call_target="tpu_custom_call" | custom-call | tf_op jit(solution)/shard_map/pallas_call | solution.py:831
  377.8 124.5 %shard_map.153 = (f32[128,640]{1,0:T(8,128)}, f32[640,256]{1,0:T(8,128)}, f32[256,640]{1,0:T(8,128)}, bf16[3,2560,256]{2,1,0:T(8,128)(2,1)}, f32[40,128]{1,0:T(8,128)}, /*index=5*/bf16[2,64,2048]{2,1,0:T(8,128)(2,1)}) custom-call(f32[1,4224]{1,0:T(1,128)} %get-tuple-element.55.refs_0_, bf16[2,64,2048]{2,1,0:T(8,128)(2,1)} %get-tuple-element.56.refs_1_, ...), custom_call_target="tpu_custom_call" | custom-call | tf_op jit(solution)/shard_map/pallas_call | solution.py:831
  502.3 0.0 copy-start.2
  502.3 0.0 copy-start.3
  502.3 0.9 dynamic_slice.3
  503.2 0.6 broadcast_in_dim.56
  503.8 0.0 copy-start.1
  503.8 6.4 %shard_map.154 = (f32[256,2,2560]{2,1,0:T(2,128)}, f32[2560,256]{1,0:T(8,128)}) custom-call(bf16[3,2560,256]{2,1,0:T(8,128)(2,1)} %get-tuple-element.96.source), custom_call_target="tpu_custom_call" | custom-call | tf_op jit(solution)/shard_map/pallas_call | solution.py:2035
  510.2 0.0 copy-start.4
  510.2 0.0 copy-start
  510.2 0.0 copy-done.2
  510.2 0.8 copy.23
  511.0 0.0 copy-done.3
  511.0 0.8 copy.24
  511.8 0.0 copy-done.1
  511.8 0.8 copy.25
  512.6 0.0 copy-done.4
  512.6 0.7 copy.26
  513.4 0.0 copy-done
  513.4 0.8 copy.27
  (5 shorter events, 0.0 us)
Async XLA Ops:
  502.3 7.9 %copy-start.2 = (bf16[2,64,2048]{2,1,0:T(8,128)(2,1)S(1)}, bf16[2,64,2048]{2,1,0:T(8,128)(2,1)}, u32[]{:S(2)}) copy-start(bf16[2,64,2048]{2,1,0:T(8,128)(2,1)} %get-tuple-element.54) | copy-start | bytes 1572868
  502.3 8.7 %copy-start.3 = (bf16[2,64,2048]{2,1,0:T(8,128)(2,1)S(1)}, bf16[2,64,2048]{2,1,0:T(8,128)(2,1)}, u32[]{:S(2)}) copy-start(bf16[2,64,2048]{2,1,0:T(8,128)(2,1)} %get-tuple-element.92) | copy-start | bytes 1572868
  503.8 8.0 %copy-start.1 = (f32[256,640]{1,0:T(8,128)S(1)}, f32[256,640]{1,0:T(8,128)}, u32[]{:S(2)}) copy-start(f32[256,640]{1,0:T(8,128)} %get-tuple-element.93) | copy-start | bytes 1966084
  510.2 2.4 copy-start.4
  510.2 3.2 copy-start

commit v3 on v2

--- a/solution.py
+++ b/solution.py
@@ -1369,7 +1369,7 @@
 
 
 WEIGHTS = ("keyval", "query", "out", "ffn")
-SCHEDULE = "bbbsbbbbrfbfbfbfbfbfbffbffbbbofff"
+SCHEDULE = "sbbbrfbfbbfbfbfbfbffbffbfbfbbbbof"
 NEIGHBOURS = (C_BIT, X_BIT, Y_BIT, Z_BIT)
 AWAY = (X_BIT | Y_BIT, X_BIT, Y_BIT)
 

time: 519 us -> 510 us (0.983); the launches traced: 514 us -> 500 us
  Pallas kernels: 496 us -> 482 us
    pallas_call x2, Pallas kernels: 490 us -> 476 us  [run(): pl.pallas_call(kernel, out_shape=tuple((jax.ShapeDtypeStruct(leaf.shape,...]
where the time goes in v3:
time: 510 us; the launch traced here: 500 us
  Pallas kernels  482 us (95%)
  local copies, waits for them, and re-layouts  15.1 us (3%)
    pallas_call x2, Pallas kernels, run(): pl.pallas_call(kernel, out_shape=tuple((jax.ShapeDtypeStruct(leaf.shape,...  476 us
    unnamed x16, local copies, waits for them, and re-layouts  11.3 us

profile of v3, /device:TPU:0, one launch (start us, length us, event | category | flops | bytes accessed | tf_op | source)
XLA Modules:
  0.0 500.2 jit_solution(16515648835720439366)
XLA Ops:
  0.7 0.1 iota_add_fusion
  0.7 0.8 select_reduce_fusion
  1.6 0.1 add_convert_fusion.1
  1.6 0.1 add.88
  1.7 1.3 pad.4.refs_3_
  3.0 0.1 add.82
  3.1 0.1 add.83
  3.1 0.6 add_convert_fusion.refs_8_.refs_43_
  3.8 0.1 broadcast_in_dim.48
  3.8 0.3 multiply_sine_fusion
  4.2 0.8 concatenate.3.refs_9_.refs_44_
  4.9 7.3 %copy.17 = bf16[1,256,2,2560]{1,3,2,0:T(8,128)(2,1)} copy(bf16[1,256,2,2560]{3,2,1,0:T(2,128)(2,1)} %param.15) | data formatting | bytes 5242880 | tf_op args[6]
  12.3 351.0 %shard_map.152 = (bf16[64,2048]{1,0:T(8,128)(2,1)}, bf16[64,2048]{1,0:T(8,128)(2,1)}, bf16[8,64,2048]{2,1,0:T(8,128)(2,1)}, bf16[1280,512]{1,0:T(8,128)(2,1)}, b...) custom-call(bf16[2,64,2048]{2,1,0:T(8,128)(2,1)} %refs_0_.1, ...), custom_call_target="tpu_custom_call" | custom-call | tf_op jit(solution)/shard_map/pallas_call | solution.py:831
  363.3 124.6 %shard_map.153 = (f32[128,640]{1,0:T(8,128)}, f32[640,256]{1,0:T(8,128)}, f32[256,640]{1,0:T(8,128)}, bf16[3,2560,256]{2,1,0:T(8,128)(2,1)}, f32[40,128]{1,0:T(8,128)}, /*index=5*/bf16[2,64,2048]{2,1,0:T(8,128)(2,1)}) custom-call(f32[1,4224]{1,0:T(1,128)} %get-tuple-element.55.refs_0_, bf16[2,64,2048]{2,1,0:T(8,128)(2,1)} %get-tuple-element.56.refs_1_, ...), custom_call_target="tpu_custom_call" | custom-call | tf_op jit(solution)/shard_map/pallas_call | solution.py:831
  487.9 0.0 copy-start.2
  487.9 0.0 copy-start.3
  487.9 0.9 dynamic_slice.3
  488.8 0.6 broadcast_in_dim.56
  489.3 0.0 copy-start.1
  489.3 6.4 %shard_map.154 = (f32[256,2,2560]{2,1,0:T(2,128)}, f32[2560,256]{1,0:T(8,128)}) custom-call(bf16[3,2560,256]{2,1,0:T(8,128)(2,1)} %get-tuple-element.96.source), custom_call_target="tpu_custom_call" | custom-call | tf_op jit(solution)/shard_map/pallas_call | solution.py:2035
  495.8 0.0 copy-start.4
  495.8 0.0 copy-start
  495.8 0.0 copy-done.2
  495.8 0.8 copy.23
  496.6 0.0 copy-done.3
  496.6 0.8 copy.24
  497.4 0.0 copy-done.1
  497.4 0.8 copy.25
  498.2 0.0 copy-done.4
  498.2 0.7 copy.26
  498.9 0.0 copy-done
  498.9 0.8 copy.27
  (5 shorter events, 0.0 us)
Async XLA Ops:
  487.9 7.9 %copy-start.2 = (bf16[2,64,2048]{2,1,0:T(8,128)(2,1)S(1)}, bf16[2,64,2048]{2,1,0:T(8,128)(2,1)}, u32[]{:S(2)}) copy-start(bf16[2,64,2048]{2,1,0:T(8,128)(2,1)} %get-tuple-element.54) | copy-start | bytes 1572868
  487.9 8.7 %copy-start.3 = (bf16[2,64,2048]{2,1,0:T(8,128)(2,1)S(1)}, bf16[2,64,2048]{2,1,0:T(8,128)(2,1)}, u32[]{:S(2)}) copy-start(bf16[2,64,2048]{2,1,0:T(8,128)(2,1)} %get-tuple-element.92) | copy-start | bytes 1572868
  489.3 8.0 %copy-start.1 = (f32[256,640]{1,0:T(8,128)S(1)}, f32[256,640]{1,0:T(8,128)}, u32[]{:S(2)}) copy-start(f32[256,640]{1,0:T(8,128)} %get-tuple-element.93) | copy-start | bytes 1966084
  495.8 2.4 copy-start.4
  495.8 3.2 copy-start
